TPU v7x, 768 devices: a whole 4x8x12 slice. The times are simulated.
768 devices in a mesh: rep: 12 (over z_lo, x), fsdp: 64 (over y, z_hi, core).
Axes of the slice: x: 4, y: 8, z: 12 (z_hi: 4, z_lo: 3; z = z_hi * 3 + z_lo), core: 2. Of those that a mesh axis runs over, the one named last changes fastest.
Arguments:
- global_weights: bfloat16 [6144, 8192], P('fsdp'), as said below
- local_weights: bfloat16 [12, 6144, 8192], P('rep', 'fsdp'), as said below
- outer_momentum: float32 [6144, 8192], P(('fsdp', 'rep')), may hold values from -6 to 6
- outer_step: int32 [12], P('rep'), may hold values from 0 to 49
Outputs:
- new_global: bfloat16 [6144, 8192], P('fsdp')
- new_momentum: float32 [6144, 8192], P(('fsdp', 'rep'))
- mixed_local: bfloat16 [12, 6144, 8192], P('rep', 'fsdp')
Inputs may be any that keep to these rules, and one draw needn't show every extreme that they name: Every entry of local_weights[r] - global_weights lies between -1000 and 1000. `global_weights`: weights of order one.
All inputs are finite; a program needn't handle non-finite values.
Results may differ from a plain program's by a relative error of at most 0.0024.
Values may be sent and summed in bfloat16 or wider, within the bound.
No kernel may reach another device: no remote copies, remote signals or barrier semaphores. Data moves between devices by JAX's collectives and lax.ppermute only.
A program may use at most 32 MiB of HBM per device.

v0:
```python
import jax
import jax.numpy as jnp
import numpy as np
from jax import lax
from jax.sharding import PartitionSpec as P

BLOCK = 128


def power_table():
    return jnp.asarray(2.0 ** np.arange(-24, 16), jnp.float32)


def block_scale(blocks):
    largest = jnp.max(jnp.abs(blocks), axis=2)
    powers = power_table()
    candidates = jnp.where(
        powers[None, None, :] >= largest[:, :, None], powers[None, None, :], powers[-1]
    )
    return jnp.min(candidates, axis=2)


def quantize(values):
    magnitude = jnp.abs(values)
    rounded = jnp.zeros_like(magnitude)
    for power in range(6, -1, -1):
        threshold = 2.0 ** (-7) if power == 6 else 0.75 * 2.0 ** (-power)
        rounded = jnp.where(magnitude >= threshold, 2.0 ** (-power), rounded)
    return jnp.sign(values) * rounded


def shards(global_weights, local_weights, outer_momentum, outer_step):
    replicas = lax.axis_size("rep")
    rows_dev, width = global_weights.shape
    share = rows_dev // replicas
    delta = global_weights.astype(jnp.float32) - local_weights[0].astype(jnp.float32)
    blocks = delta.reshape(rows_dev, width // BLOCK, BLOCK)
    scale = block_scale(blocks)
    codes = quantize(blocks / scale[:, :, None]).astype(jnp.bfloat16)
    decoded = (codes.astype(jnp.float32) * scale[:, :, None]).reshape(rows_dev, width)
    total = lax.psum_scatter(
        decoded.astype(jnp.bfloat16), "rep", scatter_dimension=0, tiled=True
    ).astype(jnp.float32)
    average = total / replicas
    squares = lax.psum(jnp.sum(average * average), ("rep", "fsdp"))
    entries = jnp.float32(rows_dev * lax.axis_size("fsdp") * width)
    factor = 0.5 / jnp.sqrt(squares / entries + 1e-06)
    clipped = factor * average
    new_momentum = 0.9 * outer_momentum + clipped
    owned = lax.dynamic_slice_in_dim(global_weights, lax.axis_index("rep") * share, share, 0)
    new_share = (owned.astype(jnp.float32) - 0.7 * (clipped + 0.9 * new_momentum)).astype(
        jnp.bfloat16
    )
    new_global = lax.all_gather(new_share, "rep", axis=0, tiled=True)
    alpha = 0.9 / (1.0 + 0.1 * outer_step[0].astype(jnp.float32))
    mixed_local = (
        alpha * local_weights.astype(jnp.float32)
        + (1.0 - alpha) * new_global.astype(jnp.float32)[None]
    ).astype(jnp.bfloat16)
    return (new_global, new_momentum, mixed_local)


def solution(mesh):
    placed = (P("fsdp", None), P("rep", "fsdp", None), P(("fsdp", "rep"), None), P("rep"))
    return jax.shard_map(
        shards,
        mesh=mesh,
        in_specs=placed,
        out_specs=(P("fsdp", None), P(("fsdp", "rep"), None), P("rep", "fsdp", None)),
        check_vma=False,
    )
```

profile of v0, /device:TPU:192, one launch (start us, length us, event | category | flops | bytes accessed | tf_op | source)
XLA Modules:
  0.0 289.7 jit_solution(16489272939372414384)
XLA Ops:
  7.2 0.0 reduce-scatter.2.cloned.1.call-start
  7.2 2.4 abs_bitcast_fusion
  9.6 2.2 copy.11
  11.8 0.0 copy-start.4
  11.8 0.0 copy-start
  11.8 0.0 copy-start.1
  11.8 2.9 %reduce_max.9 = f32[96,64]{1,0:T(8,128)S(1)} reduce(f32[96,64,128]{2,1,0:T(8,128)} %bitcast.24, f32[]{:T(128)} %constant.13.clone.1), dimensions={2}, to_apply=%region_0.0 | reduce | flops 780288 | bytes 3170308 | tf_op jit(solution)/shard_map/reduce_max | solution.py:15
  14.7 0.1 copy.9
  14.8 0.0 copy-done.4
  14.8 0.4 select_reduce_fusion
  15.2 0.1 copy.10
  15.3 0.9 div.27
  16.2 0.0 copy-done
  16.2 0.0 copy-done.1
  16.2 0.0 copy-start.3
  16.2 4.8 %fusion.3 = bf16[96,8192]{1,0:T(8,128)(2,1)} fusion(f32[12,8,64,128]{3,2,1,0:T(8,128)S(1)} %bitcast.25, bf16[1,96,8192]{2,1,0:T(8,128)(2,1)S(1)} %copy-done, bf16[96,8192]{1,0:T(8,128)(2,1)S(1)} %copy-done.1), kind=kLoop, calls=%fused_computation.7 | loop fusion | flops 19660800 | bytes 7864320 | tf_op jit(solution)/shard_map/convert_element_type | solution.py:42
  20.9 0.0 reduce-scatter.2.cloned.1.call-update
  21.0 0.0 all-gather.2.cloned.1.call-start
  21.0 80.6 %reduce-scatter.2.cloned.1.call-done = bf16[8,8192]{1,0:T(8,128)(2,1)} async-done(((bf16[96,8192]{1,0:T(8,128)(2,1)}), bf16[8,8192]{1,0:T(8,128)(2,1)}) %reduce-scatter.2.cloned.1.call-update) | async-done | bytes 131088 | tf_op jit(solution)/shard_map/reduce_scatter | solution.py:41
  101.7 1.6 fusion.10
  103.3 103.0 %psum.7 = f32[]{:T(128)} all-reduce(f32[]{:T(128)} %fusion.10), channel_id=1, replica_groups=mesh['rep'=12,'fsdp'=64] {'rep','fsdp'}, use_global_device_ids=true, to_apply=%region_4.5 | all-reduce | flops 1 | bytes 8 | tf_op jit(solution)/shard_map/psum | solution.py:45
  207.0 0.0 copy-done.3
  207.0 1.7 fusion.8
  208.7 0.0 all-gather.2.cloned.1.call-update
  209.4 69.1 %all-gather.2.cloned.1.call-done = bf16[96,8192]{1,0:T(8,128)(2,1)} async-done(((bf16[8,8192]{1,0:T(8,128)(2,1)}), bf16[96,8192]{1,0:T(8,128)(2,1)}) %all-gather.2.cloned.1.call-update) | async-done | bytes 1572880 | tf_op jit(solution)/shard_map/all_gather | solution.py:54
  278.5 0.0 copy-start.2
  278.5 3.2 %fusion.2 = bf16[1,96,8192]{2,1,0:T(8,128)(2,1)} fusion(bf16[1,96,8192]{2,1,0:T(8,128)(2,1)S(1)} %copy-done, bf16[96,8192]{1,0:T(8,128)(2,1)} %all-gather.2.cloned.1.call-done, f32[]{:T(128)S(6)} %sub.11, f32[]{:T(128)} %bitcast.1), kind=kLoop, calls=%fused_computation.4 | loop fusion | flops 4718592 | bytes 4718600 | tf_op jit(solution)/shard_map/convert_element_type | solution.py:59
  281.7 0.0 copy-done.2
  281.7 1.1 copy.16
Async XLA Ops:
  7.2 94.5 %reduce-scatter.2.cloned.1.call-start = ((), (), s32[]{:S(2)}) async-start(), calls=%async_computation.1 | async-start | bytes 1703936 | tf_op jit(solution)/shard_map/reduce_scatter | solution.py:41
  11.8 3.0 %copy-start.4 = (f32[40]{0:T(128)S(1)}, f32[40]{0:T(128)}, u32[]{:S(2)}) copy-start(f32[40]{0:T(128)} %constant.70.clone) | copy-start | bytes 484
  11.8 4.4 %copy-start = (bf16[1,96,8192]{2,1,0:T(8,128)(2,1)S(1)}, bf16[1,96,8192]{2,1,0:T(8,128)(2,1)}, u32[]{:S(2)}) copy-start(bf16[1,96,8192]{2,1,0:T(8,128)(2,1)} %param.6) | copy-start | bytes 4718596
  11.8 4.4 %copy-start.1 = (bf16[96,8192]{1,0:T(8,128)(2,1)S(1)}, bf16[96,8192]{1,0:T(8,128)(2,1)}, u32[]{:S(2)}) copy-start(bf16[96,8192]{1,0:T(8,128)(2,1)} %param.5) | copy-start | bytes 4718596
  16.2 190.8 %copy-start.3 = (f32[8,8192]{1,0:T(8,128)S(1)}, f32[8,8192]{1,0:T(8,128)}, u32[]{:S(2)}) copy-start(f32[8,8192]{1,0:T(8,128)} %param.7) | copy-start | bytes 786436
  21.0 257.5 %all-gather.2.cloned.1.call-start = ((), (), s32[]{:S(2)}) async-start(), calls=%async_computation.2 | async-start | bytes 1703936 | tf_op jit(solution)/shard_map/all_gather | solution.py:54
  278.5 3.2 %copy-start.2 = (bf16[96,8192]{1,0:T(8,128)(2,1)S(1)}, bf16[96,8192]{1,0:T(8,128)(2,1)}, u32[]{:S(2)}) copy-start(bf16[96,8192]{1,0:T(8,128)(2,1)} %all-gather.2.cloned.1.call-done) | copy-start | bytes 4718596
Sparse Core Ops, SparseCore 0:
  21.1 80.5 reduce-scatter.1
  208.8 69.6 all-gather.1
where the time goes:
time: 290 us
  waiting for transfers between devices  150 us (52%)
  blocking collectives  103 us (36%)
  other arithmetic  17 us (6%)
  between operations  15.5 us (5%)
  local copies, waits for them, and re-layouts  4.41 us (2%)
    psum x1, blocking collectives, shards(): squares = lax.psum(jnp.sum(average * average), ('rep', 'fsdp'))  103 us
    reduce_scatter x1, waiting for transfers between devices, shards(): lax.psum_scatter(decoded.astype(jnp.bfloat16), 'rep', scatter_dimension=0...  80.6 us
    all_gather x1, waiting for transfers between devices, shards(): new_global = lax.all_gather(new_share, 'rep', axis=0, tiled=True)  69.1 us
  transfers between devices with their start and end apart: 2, of which 2 were waited for; matrix products, arithmetic and copies ran while one was open for 0% of the time, Pallas kernels for 0%

commit v1 on v0

v1 whole, which is shorter than its diff:
```python
import functools

import jax
import jax.numpy as jnp
from jax import lax
from jax.experimental import pallas as pl
from jax.experimental.pallas import tpu as pltpu
from jax.sharding import PartitionSpec as P

BLOCK = 128
SPLIT = 2.0**23 + 1.0


def one_bit(values):
    wide = values * SPLIT
    near = wide - (wide - values)
    return jnp.where(values >= 1.5 * near, near + near, near)


def quantize_kernel(global_ref, local_ref, decoded_ref):
    for start in range(0, global_ref.shape[1], BLOCK):
        lanes = pl.ds(start, BLOCK)
        delta = global_ref[:, lanes].astype(jnp.float32) - local_ref[:, lanes].astype(jnp.float32)
        magnitude = jnp.abs(delta)
        largest = jnp.maximum(jnp.max(magnitude, axis=1, keepdims=True), 2.0**-24)
        near = one_bit(largest)
        scale = jnp.minimum(jnp.where(near >= largest, near, near + near), 2.0**15)
        least = scale * 2.0**-7
        level = jnp.maximum(one_bit(magnitude), least + least)
        level = jnp.where(magnitude >= least, level, 0.0)
        decoded_ref[:, lanes] = jnp.where(delta < 0.0, -level, level).astype(jnp.bfloat16)


def quantize(global_weights, local_weights):
    rows, width = global_weights.shape
    tile = 16
    block = pl.BlockSpec((tile, width), lambda i: (i, 0))
    return pl.pallas_call(
        quantize_kernel,
        out_shape=jax.ShapeDtypeStruct((rows, width), jnp.bfloat16),
        grid=(rows // tile,),
        in_specs=[block, block],
        out_specs=block,
    )(global_weights, local_weights)


def exchange_sum(value, axis, groups, count):
    copies = jnp.broadcast_to(value[None], (count,) + value.shape)
    parts = lax.all_to_all(copies, axis, 0, 0, tiled=True, axis_index_groups=groups)
    return jnp.sum(parts, axis=0)


def total_over_devices(value, replicas, peers):
    value = exchange_sum(value, "rep", None, replicas)
    inner = 8
    outer = peers // inner
    near = [[i * inner + j for j in range(inner)] for i in range(outer)]
    far = [[i * inner + j for i in range(outer)] for j in range(inner)]
    value = exchange_sum(value, "fsdp", near, inner)
    return exchange_sum(value, "fsdp", far, outer)


def shards(global_weights, local_weights, outer_momentum, outer_step):
    replicas = lax.axis_size("rep")
    peers = lax.axis_size("fsdp")
    rows_dev, width = global_weights.shape
    share = rows_dev // replicas
    decoded = quantize(global_weights, local_weights[0])
    parts = lax.all_to_all(
        decoded.reshape(replicas, share, width), "rep", 0, 0, tiled=True
    )
    average = jnp.sum(parts.astype(jnp.float32), axis=0) / replicas
    partial = jnp.sum((average * average).reshape(share, width // BLOCK, BLOCK), axis=1)
    squares = jnp.sum(total_over_devices(partial, replicas, peers))
    entries = jnp.float32(rows_dev * peers * width)
    factor = 0.5 / jnp.sqrt(squares / entries + 1e-06)
    clipped = factor * average
    new_momentum = 0.9 * outer_momentum + clipped
    owned = lax.dynamic_slice_in_dim(global_weights, lax.axis_index("rep") * share, share, 0)
    new_share = (owned.astype(jnp.float32) - 0.7 * (clipped + 0.9 * new_momentum)).astype(
        jnp.bfloat16
    )
    new_global = lax.all_to_all(
        jnp.broadcast_to(new_share[None], (replicas, share, width)), "rep", 0, 0, tiled=True
    ).reshape(rows_dev, width)
    alpha = 0.9 / (1.0 + 0.1 * outer_step[0].astype(jnp.float32))
    mixed_local = (
        alpha * local_weights.astype(jnp.float32)
        + (1.0 - alpha) * new_global.astype(jnp.float32)[None]
    ).astype(jnp.bfloat16)
    return (new_global, new_momentum, mixed_local)


def solution(mesh):
    placed = (P("fsdp", None), P("rep", "fsdp", None), P(("fsdp", "rep"), None), P("rep"))
    return jax.shard_map(
        shards,
        mesh=mesh,
        in_specs=placed,
        out_specs=(P("fsdp", None), P(("fsdp", "rep"), None), P("rep", "fsdp", None)),
        check_vma=False,
    )
```

time: 290 us -> 131 us (0.45)
  the two profiles are of different devices: /device:TPU:192 before, /device:TPU:64 now
where the time goes in v1:
time: 131 us
  blocking collectives  69.2 us (53%)
  waiting for transfers between devices  33.4 us (25%)
  starting transfers between devices  12.6 us (10%)
  Pallas kernels  6.38 us (5%)
  other arithmetic  4.31 us (3%)
  local copies, waits for them, and re-layouts  3.06 us (2%)
  between operations  2.04 us (2%)
    all_to_all x2, blocking collectives, exchange_sum(): lax.all_to_all(copies, axis, 0, 0, tiled=True, axis_index_groups=groups)  34.8 us
    all_to_all x1, blocking collectives, shards(): lax.all_to_all(decoded.reshape(replicas, share, width), 'rep', 0, 0, tile...  34.5 us
    all_to_all x1, waiting for transfers between devices, shards(): lax.all_to_all(jnp.broadcast_to(new_share[None], (replicas, share, width)...  25.3 us
    all_to_all x1, waiting for transfers between devices, exchange_sum(): lax.all_to_all(copies, axis, 0, 0, tiled=True, axis_index_groups=groups)  8.03 us
    all_to_all x1, starting transfers between devices, exchange_sum(): lax.all_to_all(copies, axis, 0, 0, tiled=True, axis_index_groups=groups)  7.1 us
    pallas_call x1, Pallas kernels, quantize(): pl.pallas_call(quantize_kernel, out_shape=jax.ShapeDtypeStruct((rows, wid...  6.38 us
    all_to_all x1, starting transfers between devices, shards(): lax.all_to_all(jnp.broadcast_to(new_share[None], (replicas, share, width)...  5.45 us
  transfers between devices with their start and end apart: 2, of which 2 were waited for; matrix products, arithmetic and copies ran while one was open for 0% of the time, Pallas kernels for 0%

profile of v1, /device:TPU:64, one launch (start us, length us, event | category | flops | bytes accessed | tf_op | source)
XLA Modules:
  0.0 130.9 jit_solution(10425526507662692510)
XLA Ops:
  0.6 6.4 %shard_map.67 = bf16[96,8192]{1,0:T(8,128)(2,1)} custom-call(bf16[96,8192]{1,0:T(8,128)(2,1)} %global_ref.1, bf16[96,8192]{1,0:T(8,128)(2,1)} %bitcast.11), custom_call_target="tpu_custom_call" | custom-call | tf_op jit(solution)/shard_map/pallas_call | solution.py:38
  7.0 34.5 %all_to_all.25 = bf16[12,8,8192]{2,1,0:T(8,128)(2,1)S(1)} all-to-all(bf16[12,8,8192]{2,1,0:T(8,128)(2,1)} %bitcast.12), channel_id=1, replica_groups=mesh['rep'=12,'fsdp'=64] {'rep'}, dimensions={0} | all-to-all | bytes 3145728 | tf_op jit(solution)/shard_map/all_to_all | solution.py:69
  41.5 0.0 copy-start.1
  41.5 0.2 convert_reduce_fusion
  41.7 0.1 bitcast_reduce_fusion
  41.8 9.7 %all_to_all.26 = f32[12,8,128]{2,1,0:T(8,128)S(1)} all-to-all(f32[12,8,128]{2,1,0:T(8,128)S(1)} %broadcast_in_dim.8), channel_id=1, replica_groups=mesh['rep'=12,'fsdp'=64] {'rep'}, dimensions={0} | all-to-all | bytes 98304 | tf_op jit(solution)/shard_map/all_to_all | solution.py:49
  51.5 25.1 %all_to_all.27 = f32[8,8,128]{2,1,0:T(8,128)S(1)} all-to-all(f32[8,8,128]{2,1,0:T(8,128)S(1)} %broadcast_in_dim.9), channel_id=1, replica_groups={{0,1,2,3,4,5,6,7},{8,9,10,11,12,13,14,15},{16,17,18,19,20,21,22,23},{24..., dimensions={0} | all-to-all | bytes 65536 | tf_op jit(solution)/shard_map/all_to_all | solution.py:49
  76.6 0.6 broadcast_in_dim.10
  77.2 7.1 %all-to-all-start.3 = ((f32[8,8,128]{2,1,0:T(8,128)}), f32[8,8,128]{2,1,0:T(8,128)S(1)}, u32[]{:S(2)}, u32[]{:S(2)}) async-start(f32[8,8,128]{2,1,0:T(8,128)} %broadcast_in_dim.10), calls=%async_computation.3 | async-start | bytes 65536 | tf_op jit(solution)/shard_map/all_to_all | solution.py:49
  84.3 8.0 %all-to-all-done.3 = f32[8,8,128]{2,1,0:T(8,128)S(1)} async-done(((f32[8,8,128]{2,1,0:T(8,128)}), f32[8,8,128]{2,1,0:T(8,128)S(1)}, u32[]{:S(2)}, u32[]{:S(2)}) %all-to-all-start.3) | async-done | bytes 32800 | tf_op jit(solution)/shard_map/all_to_all | solution.py:49
  92.3 0.6 reduce_sum.53
  93.6 0.0 copy-done.1
  93.6 1.7 %subtract_convert_fusion = (bf16[8,8192]{1,0:T(8,128)(2,1)S(1)}, f32[8,8192]{1,0:T(8,128)}) fusion(f32[8,8192]{1,0:T(8,128)S(1)} %convert_reduce_fusion, f32[]{:T(128)S(6)} %mul.56, bf16[96,8192]{1,0:T(8,128)(2,1)} %global_ref.1, s32[]{:T(128)S(6)} %select_n.3, f32[8,8192]{1,0:T(8,128)S(1)} %copy-done.1), kind=kLoop, calls=%fused_computation.4 | loop fusion | flops 589824 | bytes 1048584 | tf_op jit(solution)/shard_map/convert_element_type | solution.py:80
  95.3 1.3 broadcast_in_dim.11
  96.6 0.0 copy-start
  96.6 5.5 %all-to-all-start.4 = ((bf16[12,8,8192]{2,1,0:T(8,128)(2,1)}), bf16[12,8,8192]{2,1,0:T(8,128)(2,1)S(1)}, u32[]{:S(2)}, u32[]{:S(2)}) async-start(bf16[12,8,8192]{2,1,0:T(8,128)(2,1)} %broadcast_in_dim.11), calls=%async_computation.4 | async-start | bytes 3145728 | tf_op jit(solution)/shard_map/all_to_all | solution.py:83
  102.8 25.3 %all-to-all-done.4 = bf16[12,8,8192]{2,1,0:T(8,128)(2,1)S(1)} async-done(((bf16[12,8,8192]{2,1,0:T(8,128)(2,1)}), bf16[12,8,8192]{2,1,0:T(8,128)(2,1)S(1)}, u32[]{:S(2)}, u32[]{:S(2)}) %all-to-all-start.4) | async-done | bytes 1572896 | tf_op jit(solution)/shard_map/all_to_all | solution.py:83
  128.1 0.0 copy-done
  128.1 1.7 %fusion = bf16[1,96,8192]{2,1,0:T(8,128)(2,1)} fusion(bf16[12,8,8192]{2,1,0:T(8,128)(2,1)S(1)} %all-to-all-done.4, bf16[1,96,8192]{2,1,0:T(8,128)(2,1)S(1)} %copy-done, f32[]{:T(128)S(6)} %sub.7, f32[]{:T(128)} %bitcast.4), kind=kLoop, calls=%fused_computation.1 | loop fusion | flops 4718592 | bytes 4718600 | tf_op jit(solution)/shard_map/convert_element_type | solution.py:90
  129.8 1.1 copy.9
  (4 shorter events, 0.0 us)
Async XLA Ops:
  41.5 52.2 %copy-start.1 = (f32[8,8192]{1,0:T(8,128)S(1)}, f32[8,8192]{1,0:T(8,128)}, u32[]{:S(2)}) copy-start(f32[8,8192]{1,0:T(8,128)} %param.6) | copy-start | bytes 786436
  77.2 15.1 %all-to-all-start.3 = ((f32[8,8,128]{2,1,0:T(8,128)}), f32[8,8,128]{2,1,0:T(8,128)S(1)}, u32[]{:S(2)}, u32[]{:S(2)}) async-start(f32[8,8,128]{2,1,0:T(8,128)} %broadcast_in_dim.10), calls=%async_computation.3 | async-start | bytes 65536 | tf_op jit(solution)/shard_map/all_to_all | solution.py:49
  96.6 31.5 %copy-start = (bf16[1,96,8192]{2,1,0:T(8,128)(2,1)S(1)}, bf16[1,96,8192]{2,1,0:T(8,128)(2,1)}, u32[]{:S(2)}) copy-start(bf16[1,96,8192]{2,1,0:T(8,128)(2,1)} %param.5) | copy-start | bytes 4718596
  96.6 31.5 %all-to-all-start.4 = ((bf16[12,8,8192]{2,1,0:T(8,128)(2,1)}), bf16[12,8,8192]{2,1,0:T(8,128)(2,1)S(1)}, u32[]{:S(2)}, u32[]{:S(2)}) async-start(bf16[12,8,8192]{2,1,0:T(8,128)(2,1)} %broadcast_in_dim.11), calls=%async_computation.4 | async-start | bytes 3145728 | tf_op jit(solution)/shard_map/all_to_all | solution.py:83

commit v2 on v1

v2 whole, which is shorter than its diff:
```python
import functools
import itertools

import jax
import jax.numpy as jnp
from jax import lax
from jax.experimental import pallas as pl
from jax.experimental.pallas import tpu as pltpu
from jax.sharding import PartitionSpec as P

BLOCK = 128
SPLIT = 2.0**23 + 1.0
VMEM = pltpu.CompilerParams(vmem_limit_bytes=24 * 2**20)
WHOLE = pl.BlockSpec(memory_space=pltpu.VMEM)


def one_bit(values):
    wide = values * SPLIT
    return wide - (wide - values)


def quantize_kernel(global_ref, local_ref, decoded_ref, global_tile, local_tile, decoded_tile, arrived, sent):
    step = 16
    count = global_ref.shape[0] // step

    def tile_rows(i):
        return pl.ds(pl.multiple_of(i * step, step), step)

    def fetch(i):
        return [
            pltpu.make_async_copy(ref.at[tile_rows(i)], tile.at[tile_rows(i)], arrived.at[k, i])
            for k, (ref, tile) in enumerate(((global_ref, global_tile), (local_ref, local_tile)))
        ]

    def put(i):
        return pltpu.make_async_copy(decoded_tile.at[tile_rows(i)], decoded_ref.at[tile_rows(i)], sent.at[i])

    for i in range(count):
        for copy in fetch(i):
            copy.start()

    @pl.loop(0, count)
    def _(i):
        for copy in fetch(i):
            copy.wait()
        for start in range(0, global_ref.shape[1], BLOCK):
            at = (tile_rows(i), pl.ds(start, BLOCK))
            delta = global_tile[at].astype(jnp.float32) - local_tile[at].astype(jnp.float32)
            magnitude = jnp.abs(delta)
            largest = jnp.maximum(jnp.max(magnitude, axis=1, keepdims=True), 2.0**-24)
            near = one_bit(largest)
            scale = jnp.minimum(jnp.where(near >= largest, near, near + near), 2.0**15)
            least = scale * 2.0**-7
            level = jnp.maximum(one_bit(magnitude), least + least)
            level = jnp.where(magnitude >= least, level, 0.0)
            decoded_tile[at] = jnp.where(delta < 0.0, -level, level).astype(jnp.bfloat16)
        put(i).start()

    for i in range(count):
        put(i).wait()


def quantize(global_weights, local_weights):
    shape = global_weights.shape
    far = pl.BlockSpec(memory_space=pl.ANY)
    steps = shape[0] // 16
    return pl.pallas_call(
        quantize_kernel,
        out_shape=jax.ShapeDtypeStruct(shape, jnp.bfloat16),
        in_specs=[far, far],
        out_specs=far,
        scratch_shapes=[
            pltpu.VMEM(shape, jnp.bfloat16),
            pltpu.VMEM(shape, jnp.bfloat16),
            pltpu.VMEM(shape, jnp.bfloat16),
            pltpu.SemaphoreType.DMA((2, steps)),
            pltpu.SemaphoreType.DMA((steps,)),
        ],
    )(global_weights, local_weights)


def total_kernel(parts_ref, momentum_ref, average_ref, carried_ref, squares_ref):
    squares = jnp.zeros((parts_ref.shape[1], BLOCK), jnp.float32)
    for start in range(0, parts_ref.shape[2], BLOCK):
        lanes = pl.ds(start, BLOCK)
        total = parts_ref[0, :, lanes].astype(jnp.float32)
        for r in range(1, parts_ref.shape[0]):
            total += parts_ref[r, :, lanes].astype(jnp.float32)
        average = total / parts_ref.shape[0]
        average_ref[:, lanes] = average
        squares += average * average
        momentum = momentum_ref[:, lanes]
        coarse = momentum.astype(jnp.bfloat16)
        carried_ref[0, :, lanes] = total.astype(jnp.bfloat16)
        carried_ref[1, :, lanes] = coarse
        carried_ref[2, :, lanes] = (momentum - coarse.astype(jnp.float32)).astype(jnp.bfloat16)
    for i in range(squares_ref.shape[0]):
        squares_ref[i] = squares


def totals(parts, momentum, copies):
    share, width = momentum.shape
    return pl.pallas_call(
        total_kernel,
        out_shape=(
            jax.ShapeDtypeStruct((share, width), jnp.float32),
            jax.ShapeDtypeStruct((3, share, width), jnp.bfloat16),
            jax.ShapeDtypeStruct((copies, share, BLOCK), jnp.float32),
        ),
        in_specs=[WHOLE, WHOLE],
        out_specs=(WHOLE, WHOLE, WHOLE),
        compiler_params=VMEM,
    )(parts, momentum)


def update_kernel(
    entries, replicas, layer_ref, step_ref, parts_ref, average_ref, momentum_ref, own_ref, behind_ref, ahead_ref,
    owned_ref, new_momentum_ref, copies_ref, alpha_ref,
):
    steps = jnp.full(alpha_ref.shape, step_ref[0], jnp.int32).astype(jnp.float32)
    alpha_ref[...] = 0.9 / (1.0 + 0.1 * steps)
    squares = jnp.sum(jnp.sum(parts_ref[...], axis=0), keepdims=True)
    factor = 0.5 / jnp.sqrt(squares / entries + 1e-06)
    part = factor / replicas
    layers = owned_ref.shape[0]
    step = 512
    for start in range(0, average_ref.shape[1], step):
        lanes = pl.ds(start, step)
        new_momentum_ref[:, lanes] = 0.9 * momentum_ref[:, lanes] + factor * average_ref[:, lanes]
    for away, carried_ref in enumerate((own_ref, behind_ref, ahead_ref)):
        layer = lax.rem(layer_ref[0] + layers - away, layers)
        for start in range(0, own_ref.shape[2], step):
            lanes = pl.ds(start, step)
            total, coarse, fine = (carried_ref[i, :, lanes].astype(jnp.float32) for i in range(3))
            clipped = part * total
            new_momentum = 0.9 * (coarse + fine) + clipped
            share = (
                owned_ref[layer, :, lanes].astype(jnp.float32) - 0.7 * (clipped + 0.9 * new_momentum)
            ).astype(jnp.bfloat16)
            for i in range(copies_ref.shape[0]):
                copies_ref[i, layer, :, lanes] = share


def update(entries, replicas, layer, outer_step, parts, average, momentum, own, behind, ahead, owned, copies):
    layers, share, width = owned.shape
    return pl.pallas_call(
        functools.partial(update_kernel, entries, replicas),
        out_shape=(
            jax.ShapeDtypeStruct((share, width), jnp.float32),
            jax.ShapeDtypeStruct((copies, layers, share, width), jnp.bfloat16),
            jax.ShapeDtypeStruct((share, BLOCK), jnp.float32),
        ),
        in_specs=[pl.BlockSpec(memory_space=pltpu.SMEM)] * 2 + [WHOLE] * 7,
        out_specs=(WHOLE, WHOLE, WHOLE),
        compiler_params=VMEM,
    )(layer, outer_step, parts, average, momentum, own, behind, ahead, owned)


def mix_kernel(alpha_ref, gathered_ref, local_ref, new_global_ref, mixed_ref):
    alpha = alpha_ref[:, 0:1]
    rest = 1.0 - alpha
    for i in range(gathered_ref.shape[0]):
        for start in range(0, gathered_ref.shape[3], 1024):
            lanes = pl.ds(start, 1024)
            new_global = gathered_ref[i, 0, :, lanes]
            new_global_ref[i, :, lanes] = new_global
            mixed_ref[i, :, lanes] = (
                alpha * local_ref[i, :, lanes].astype(jnp.float32) + rest * new_global.astype(jnp.float32)
            ).astype(jnp.bfloat16)


def mix(alpha, gathered, local_weights):
    columns, layers, share, width = gathered.shape
    block = pl.BlockSpec((columns, share, width), lambda i: (i, 0, 0))
    shape = jax.ShapeDtypeStruct((layers * columns, share, width), jnp.bfloat16)
    return pl.pallas_call(
        mix_kernel,
        out_shape=(shape, shape),
        grid=(layers,),
        in_specs=[WHOLE, pl.BlockSpec((columns, 1, share, width), lambda i: (0, i, 0, 0)), block],
        out_specs=(block, block),
        compiler_params=VMEM,
    )(alpha, gathered, local_weights.reshape(shape.shape))


def grouped(lengths, inside):
    names = list(lengths)
    strides = {n: 1 for n in names}
    for n, after in zip(names[-2::-1], names[:0:-1]):
        strides[n] = strides[after] * lengths[after]
    outside = [n for n in names if n not in inside]

    def offsets(axes):
        steps = [[i * strides[n] for i in range(lengths[n])] for n in axes]
        return [sum(each) for each in itertools.product(*steps)]

    return [[a + b for b in offsets(inside)] for a in offsets(outside)]


def exchange(copies, groups):
    return lax.all_to_all(copies, ("rep", "fsdp"), 0, 0, tiled=True, axis_index_groups=groups)


def shards(global_weights, local_weights, outer_momentum, outer_step):
    replicas = lax.axis_size("rep")
    peers = lax.axis_size("fsdp")
    rows_dev, width = global_weights.shape
    share = rows_dev // replicas
    lengths = dict(z_lo=3, x=4, y=8, z_hi=4, core=2)
    layers, columns = lengths["z_lo"], lengths["x"]
    place = lax.axis_index("rep")
    owned = lax.dynamic_index_in_dim(
        global_weights.reshape(layers, columns, share, width), lax.rem(place, columns), 1, keepdims=False
    )
    plane = grouped(lengths, ("x", "y"))
    line = grouped(lengths, ("z_lo", "z_hi", "core"))
    decoded = quantize(global_weights, local_weights[0])
    parts = lax.all_to_all(
        decoded.reshape(replicas, share, width), "rep", 0, 0, tiled=True
    )
    average, carried, partial = totals(parts, outer_momentum, len(line[0]))
    behind, ahead = (
        lax.ppermute(carried, "rep", [(i, (i + away * columns) % replicas) for i in range(replicas)])
        for away in (1, 2)
    )
    partial = jnp.sum(exchange(partial, line), axis=0)
    partials = exchange(jnp.broadcast_to(partial[None], (len(plane[0]),) + partial.shape), plane)
    entries = float(rows_dev * peers * width)
    layer = (place // columns).astype(jnp.int32)[None]
    new_momentum, copies, alpha = update(
        entries, replicas, layer, outer_step, partials, average, outer_momentum, carried, behind, ahead, owned, columns
    )
    beside = [[i * columns + j for j in range(columns)] for i in range(layers)]
    gathered = lax.all_to_all(copies, "rep", 0, 0, tiled=True, axis_index_groups=beside)
    new_global, mixed_local = mix(alpha, gathered, local_weights[0])
    return (
        new_global.reshape(rows_dev, width),
        new_momentum,
        mixed_local.reshape(local_weights.shape),
    )


def solution(mesh):
    placed = (P("fsdp", None), P("rep", "fsdp", None), P(("fsdp", "rep"), None), P("rep"))
    return jax.shard_map(
        shards,
        mesh=mesh,
        in_specs=placed,
        out_specs=(P("fsdp", None), P(("fsdp", "rep"), None), P("rep", "fsdp", None)),
        check_vma=False,
    )
```

time: 131 us -> 113 us (0.86)
  the two profiles are of different devices: /device:TPU:64 before, /device:TPU:8 now
where the time goes in v2:
time: 113 us
  blocking collectives  57.1 us (51%)
  starting transfers between devices  31.1 us (28%)
  waiting for transfers between devices  12.4 us (11%)
  Pallas kernels  8.91 us (8%)
  local copies, waits for them, and re-layouts  1.71 us (2%)
  between operations  1.37 us (1%)
    all_to_all x1, blocking collectives, shards(): lax.all_to_all(decoded.reshape(replicas, share, width), 'rep', 0, 0, tile...  34.8 us
    all_to_all x2, starting transfers between devices, exchange(): lax.all_to_all(copies, ('rep', 'fsdp'), 0, 0, tiled=True, axis_index_grou...  24.5 us
    all_to_all x1, blocking collectives, shards(): lax.all_to_all(copies, 'rep', 0, 0, tiled=True, axis_index_groups=beside)  22.3 us
    all_to_all x2, waiting for transfers between devices, exchange(): lax.all_to_all(copies, ('rep', 'fsdp'), 0, 0, tiled=True, axis_index_grou...  10.5 us
    ppermute x2, starting transfers between devices, shards(): lax.ppermute(carried, 'rep', [(i, (i + away * columns) % replicas) for i...  6.58 us
    pallas_call x1, Pallas kernels, quantize(): pl.pallas_call(quantize_kernel, out_shape=jax.ShapeDtypeStruct(shape, jnp...  4.58 us
    pallas_call x1, Pallas kernels, mix(): pl.pallas_call(mix_kernel, out_shape=(shape, shape), grid=(layers,), in_s...  2.37 us
  transfers between devices with their start and end apart: 4, of which 3 were waited for; matrix products, arithmetic and copies ran while one was open for 2% of the time, Pallas kernels for 0%

profile of v2, /device:TPU:8, one launch (start us, length us, event | category | flops | bytes accessed | tf_op | source)
XLA Modules:
  0.0 112.6 jit_solution(2048656636108359354)
XLA Ops:
  0.6 4.6 %shard_map.67 = bf16[96,8192]{1,0:T(8,128)(2,1)} custom-call(bf16[96,8192]{1,0:T(8,128)(2,1)} %global_ref.1, bf16[96,8192]{1,0:T(8,128)(2,1)} %bitcast.11), custom_call_target="tpu_custom_call" | custom-call | tf_op jit(solution)/shard_map/pallas_call | solution.py:67
  5.2 0.0 copy-start.1
  5.2 34.8 %all_to_all.20.parts_ref = bf16[12,8,8192]{2,1,0:T(8,128)(2,1)S(1)} all-to-all(bf16[12,8,8192]{2,1,0:T(8,128)(2,1)} %bitcast.13), channel_id=1, replica_groups=mesh['rep'=12,'fsdp'=64] {'rep'}, dimensions={0} | all-to-all | bytes 3145728 | tf_op jit(solution)/shard_map/all_to_all | solution.py:218
  40.0 0.0 copy-done.1
  40.0 0.9 shard_map.68
  40.9 15.3 %all-to-all-start.1 = ((f32[24,8,128]{2,1,0:T(8,128)}), f32[24,8,128]{2,1,0:T(8,128)S(1)}, u32[]{:S(2)}, u32[]{:S(2)}) async-start(f32[24,8,128]{2,1,0:T(8,128)} %get-tuple-element.11), calls=%async_computation.1 | async-start | bytes 196608 | tf_op jit(solution)/shard_map/all_to_all | solution.py:201
  56.2 4.7 %collective-permute-start.1 = (bf16[3,8,8192]{2,1,0:T(8,128)(2,1)S(1)}, bf16[3,8,8192]{2,1,0:T(8,128)(2,1)S(1)}, u32[]{:S(2)}, u32[]{:S(2)}) collective-permute-start(bf16[3,8,8192]{2,1,0:T(8,128)(2,1)S(1)} %get-tuple-element.13.own_ref), channel_id=1, source_target_pairs={{0,512},{64,576},{128,640},{192,704},{256,0},{320,64},{384,128},{4... | collective-permute-start | bytes 1179656 | tf_op jit(solution)/shard_map/ppermute | solution.py:223
  60.9 1.9 %collective-permute-start = (bf16[3,8,8192]{2,1,0:T(8,128)(2,1)S(1)}, bf16[3,8,8192]{2,1,0:T(8,128)(2,1)S(1)}, u32[]{:S(2)}, u32[]{:S(2)}) collective-permute-start(bf16[3,8,8192]{2,1,0:T(8,128)(2,1)S(1)} %get-tuple-element.13.own_ref), channel_id=1, source_target_pairs={{0,256},{64,320},{128,384},{192,448},{256,512},{320,576},{384,640}... | collective-permute-start | bytes 1179656 | tf_op jit(solution)/shard_map/ppermute | solution.py:223
  62.8 4.0 %all-to-all-done.1 = f32[24,8,128]{2,1,0:T(8,128)S(1)} async-done(((f32[24,8,128]{2,1,0:T(8,128)}), f32[24,8,128]{2,1,0:T(8,128)S(1)}, u32[]{:S(2)}, u32[]{:S(2)}) %all-to-all-start.1) | async-done | bytes 98336 | tf_op jit(solution)/shard_map/all_to_all | solution.py:201
  66.9 0.7 broadcast_in_dim.10
  67.5 9.2 %all-to-all-start.2 = ((f32[32,8,128]{2,1,0:T(8,128)}), f32[32,8,128]{2,1,0:T(8,128)S(1)}, u32[]{:S(2)}, u32[]{:S(2)}) async-start(f32[32,8,128]{2,1,0:T(8,128)} %broadcast_in_dim.10), calls=%async_computation.2 | async-start | bytes 262144 | tf_op jit(solution)/shard_map/all_to_all | solution.py:201
  76.7 1.0 dynamic-slice_bitcast_fusion.owned_ref
  78.4 0.0 collective-permute-done.1.ahead_ref
  78.5 1.9 %collective-permute-done.behind_ref = bf16[3,8,8192]{2,1,0:T(8,128)(2,1)S(1)} collective-permute-done((bf16[3,8,8192]{2,1,0:T(8,128)(2,1)S(1)}, bf16[3,8,8192]{2,1,0:T(8,128)(2,1)S(1)}, u32[]{:S(2)}, u32[]{:S(2)}) %collective-permute-start) | collective-permute-done | bytes 393248 | tf_op jit(solution)/shard_map/ppermute | solution.py:223
  80.4 6.4 %all-to-all-done.2.parts_ref = f32[32,8,128]{2,1,0:T(8,128)S(1)} async-done(((f32[32,8,128]{2,1,0:T(8,128)}), f32[32,8,128]{2,1,0:T(8,128)S(1)}, u32[]{:S(2)}, u32[]{:S(2)}) %all-to-all-start.2) | async-done | bytes 131104 | tf_op jit(solution)/shard_map/all_to_all | solution.py:201
  86.8 1.1 shard_map.69
  87.9 0.0 copy-start
  87.9 22.3 %all_to_all.21.gathered_ref = bf16[4,3,8,8192]{3,2,1,0:T(8,128)(2,1)S(1)} all-to-all(bf16[4,3,8,8192]{3,2,1,0:T(8,128)(2,1)S(1)} %get-tuple-element.15), channel_id=1, replica_groups={{0,64,128,192},{256,320,384,448},{512,576,640,704},{1,65,129,193},{257,..., dimensions={0} | all-to-all | bytes 3145728 | tf_op jit(solution)/shard_map/all_to_all | solution.py:234
  110.2 0.0 copy-done
  110.2 2.4 %shard_map.70 = (bf16[12,8,8192]{2,1,0:T(8,128)(2,1)}, bf16[12,8,8192]{2,1,0:T(8,128)(2,1)}) custom-call(f32[8,128]{1,0:T(8,128)S(1)} %get-tuple-element.14.alpha_ref, bf16[4,3,8,8192]{3,2,1,0:T(8,128)(2,1)S(1)} %all_to_all.21.gathered_ref, bf16[12,8,8192]{2,1,0:T(8,128)(2,1)S(1)} %bitcast.12), custom_call_target="tpu_custom_call" | custom-call | tf_op jit(solution)/shard_map/pallas_call | solution.py:176
  (1 shorter events, 0.0 us)
Async XLA Ops:
  5.2 34.8 %copy-start.1 = (f32[8,8192]{1,0:T(8,128)S(1)}, f32[8,8192]{1,0:T(8,128)}, u32[]{:S(2)}) copy-start(f32[8,8192]{1,0:T(8,128)} %momentum_ref.3) | copy-start | bytes 786436
  40.9 25.9 %all-to-all-start.1 = ((f32[24,8,128]{2,1,0:T(8,128)}), f32[24,8,128]{2,1,0:T(8,128)S(1)}, u32[]{:S(2)}, u32[]{:S(2)}) async-start(f32[24,8,128]{2,1,0:T(8,128)} %get-tuple-element.11), calls=%async_computation.1 | async-start | bytes 196608 | tf_op jit(solution)/shard_map/all_to_all | solution.py:201
  56.2 22.2 %collective-permute-start.1 = (bf16[3,8,8192]{2,1,0:T(8,128)(2,1)S(1)}, bf16[3,8,8192]{2,1,0:T(8,128)(2,1)S(1)}, u32[]{:S(2)}, u32[]{:S(2)}) collective-permute-start(bf16[3,8,8192]{2,1,0:T(8,128)(2,1)S(1)} %get-tuple-element.13.own_ref), channel_id=1, source_target_pairs={{0,512},{64,576},{128,640},{192,704},{256,0},{320,64},{384,128},{4... | collective-permute-start | bytes 1179656 | tf_op jit(solution)/shard_map/ppermute | solution.py:223
  60.9 19.5 %collective-permute-start = (bf16[3,8,8192]{2,1,0:T(8,128)(2,1)S(1)}, bf16[3,8,8192]{2,1,0:T(8,128)(2,1)S(1)}, u32[]{:S(2)}, u32[]{:S(2)}) collective-permute-start(bf16[3,8,8192]{2,1,0:T(8,128)(2,1)S(1)} %get-tuple-element.13.own_ref), channel_id=1, source_target_pairs={{0,256},{64,320},{128,384},{192,448},{256,512},{320,576},{384,640}... | collective-permute-start | bytes 1179656 | tf_op jit(solution)/shard_map/ppermute | solution.py:223
  67.5 19.3 %all-to-all-start.2 = ((f32[32,8,128]{2,1,0:T(8,128)}), f32[32,8,128]{2,1,0:T(8,128)S(1)}, u32[]{:S(2)}, u32[]{:S(2)}) async-start(f32[32,8,128]{2,1,0:T(8,128)} %broadcast_in_dim.10), calls=%async_computation.2 | async-start | bytes 262144 | tf_op jit(solution)/shard_map/all_to_all | solution.py:201
  87.9 22.4 %copy-start = (bf16[1,96,8192]{2,1,0:T(8,128)(2,1)S(1)}, bf16[1,96,8192]{2,1,0:T(8,128)(2,1)}, u32[]{:S(2)}) copy-start(bf16[1,96,8192]{2,1,0:T(8,128)(2,1)} %param.5) | copy-start | bytes 4718596

commit v3 on v2

--- a/solution.py
+++ b/solution.py
@@ -94,6 +94,7 @@
         carried_ref[0, :, lanes] = total.astype(jnp.bfloat16)
         carried_ref[1, :, lanes] = coarse
         carried_ref[2, :, lanes] = (momentum - coarse.astype(jnp.float32)).astype(jnp.bfloat16)
+    squares = jnp.sum(squares, axis=0, keepdims=True)
     for i in range(squares_ref.shape[0]):
         squares_ref[i] = squares
 
@@ -105,7 +106,7 @@
         out_shape=(
             jax.ShapeDtypeStruct((share, width), jnp.float32),
             jax.ShapeDtypeStruct((3, share, width), jnp.bfloat16),
-            jax.ShapeDtypeStruct((copies, share, BLOCK), jnp.float32),
+            jax.ShapeDtypeStruct((copies, 1, BLOCK), jnp.float32),
         ),
         in_specs=[WHOLE, WHOLE],
         out_specs=(WHOLE, WHOLE, WHOLE),
@@ -156,29 +157,46 @@
     )(layer, outer_step, parts, average, momentum, own, behind, ahead, owned)
 
 
-def mix_kernel(alpha_ref, gathered_ref, local_ref, new_global_ref, mixed_ref):
+def mix_kernel(alpha_ref, gathered_ref, local_ref, new_global_ref, mixed_ref, mixed_tile, kept, sent):
     alpha = alpha_ref[:, 0:1]
     rest = 1.0 - alpha
-    for i in range(gathered_ref.shape[0]):
-        for start in range(0, gathered_ref.shape[3], 1024):
-            lanes = pl.ds(start, 1024)
-            new_global = gathered_ref[i, 0, :, lanes]
-            new_global_ref[i, :, lanes] = new_global
-            mixed_ref[i, :, lanes] = (
-                alpha * local_ref[i, :, lanes].astype(jnp.float32) + rest * new_global.astype(jnp.float32)
-            ).astype(jnp.bfloat16)
+    columns, layers, _, width = gathered_ref.shape
+    copies = []
+    for layer in range(layers):
+        for i in range(columns):
+            j = layer * columns + i
+            copies.append(pltpu.make_async_copy(gathered_ref.at[i, layer], new_global_ref.at[j], kept.at[j]))
+            copies[-1].start()
+    for layer in range(layers):
+        for i in range(columns):
+            j = layer * columns + i
+            for start in range(0, width, 1024):
+                lanes = pl.ds(start, 1024)
+                mixed_tile[j, :, lanes] = (
+                    alpha * local_ref[j, :, lanes].astype(jnp.float32)
+                    + rest * gathered_ref[i, layer, :, lanes].astype(jnp.float32)
+                ).astype(jnp.bfloat16)
+            copies.append(pltpu.make_async_copy(mixed_tile.at[j], mixed_ref.at[j], sent.at[j]))
+            copies[-1].start()
+    for copy in copies:
+        copy.wait()
 
 
 def mix(alpha, gathered, local_weights):
     columns, layers, share, width = gathered.shape
-    block = pl.BlockSpec((columns, share, width), lambda i: (i, 0, 0))
-    shape = jax.ShapeDtypeStruct((layers * columns, share, width), jnp.bfloat16)
+    count = layers * columns
+    shape = jax.ShapeDtypeStruct((count, share, width), jnp.bfloat16)
+    far = pl.BlockSpec(memory_space=pl.ANY)
     return pl.pallas_call(
         mix_kernel,
         out_shape=(shape, shape),
-        grid=(layers,),
-        in_specs=[WHOLE, pl.BlockSpec((columns, 1, share, width), lambda i: (0, i, 0, 0)), block],
-        out_specs=(block, block),
+        in_specs=[WHOLE, WHOLE, WHOLE],
+        out_specs=(far, far),
+        scratch_shapes=[
+            pltpu.VMEM(shape.shape, jnp.bfloat16),
+            pltpu.SemaphoreType.DMA((count,)),
+            pltpu.SemaphoreType.DMA((count,)),
+        ],
         compiler_params=VMEM,
     )(alpha, gathered, local_weights.reshape(shape.shape))
 

time: 113 us -> 110 us (0.973)
  the two profiles are of different devices: /device:TPU:8 before, /device:TPU:2 now
where the time goes in v3:
time: 110 us
  blocking collectives  56.3 us (51%)
  starting transfers between devices  31.8 us (29%)
  waiting for transfers between devices  10 us (9%)
  Pallas kernels  8.43 us (8%)
  local copies, waits for them, and re-layouts  1.66 us (2%)
  between operations  1.37 us (1%)
    all_to_all x1, blocking collectives, shards(): lax.all_to_all(decoded.reshape(replicas, share, width), 'rep', 0, 0, tile...  34.2 us
    all_to_all x2, starting transfers between devices, exchange(): lax.all_to_all(copies, ('rep', 'fsdp'), 0, 0, tiled=True, axis_index_grou...  25.2 us
    all_to_all x1, blocking collectives, shards(): lax.all_to_all(copies, 'rep', 0, 0, tiled=True, axis_index_groups=beside)  22.1 us
    all_to_all x2, waiting for transfers between devices, exchange(): lax.all_to_all(copies, ('rep', 'fsdp'), 0, 0, tiled=True, axis_index_grou...  9.99 us
    ppermute x2, starting transfers between devices, shards(): lax.ppermute(carried, 'rep', [(i, (i + away * columns) % replicas) for i...  6.58 us
    pallas_call x1, Pallas kernels, quantize(): pl.pallas_call(quantize_kernel, out_shape=jax.ShapeDtypeStruct(shape, jnp...  4.58 us
  transfers between devices with their start and end apart: 4, of which 2 were waited for; matrix products, arithmetic and copies ran while one was open for 2% of the time, Pallas kernels for 0%

profile of v3, /device:TPU:2, one launch (start us, length us, event | category | flops | bytes accessed | tf_op | source)
XLA Modules:
  0.0 109.5 jit_solution(18144069104001735858)
XLA Ops:
  0.6 4.6 %shard_map.67 = bf16[96,8192]{1,0:T(8,128)(2,1)} custom-call(bf16[96,8192]{1,0:T(8,128)(2,1)} %global_ref.1, bf16[96,8192]{1,0:T(8,128)(2,1)} %bitcast.11), custom_call_target="tpu_custom_call" | custom-call | tf_op jit(solution)/shard_map/pallas_call | solution.py:67
  5.2 0.0 copy-start.1
  5.2 34.2 %all_to_all.20.parts_ref = bf16[12,8,8192]{2,1,0:T(8,128)(2,1)S(1)} all-to-all(bf16[12,8,8192]{2,1,0:T(8,128)(2,1)} %bitcast.13), channel_id=1, replica_groups=mesh['rep'=12,'fsdp'=64] {'rep'}, dimensions={0} | all-to-all | bytes 3145728 | tf_op jit(solution)/shard_map/all_to_all | solution.py:236
  39.4 0.0 copy-done.1
  39.4 0.8 shard_map.68
  40.2 15.0 %all-to-all-start.1 = ((f32[24,1,128]{2,1,0:T(1,128)}), f32[24,1,128]{2,1,0:T(1,128)S(1)}, u32[]{:S(2)}, u32[]{:S(2)}) async-start(f32[24,1,128]{2,1,0:T(1,128)} %get-tuple-element.11), calls=%async_computation.1 | async-start | bytes 24576 | tf_op jit(solution)/shard_map/all_to_all | solution.py:219
  55.2 4.7 %collective-permute-start.1 = (bf16[3,8,8192]{2,1,0:T(8,128)(2,1)S(1)}, bf16[3,8,8192]{2,1,0:T(8,128)(2,1)S(1)}, u32[]{:S(2)}, u32[]{:S(2)}) collective-permute-start(bf16[3,8,8192]{2,1,0:T(8,128)(2,1)S(1)} %get-tuple-element.13.own_ref), channel_id=1, source_target_pairs={{0,512},{64,576},{128,640},{192,704},{256,0},{320,64},{384,128},{4... | collective-permute-start | bytes 1179656 | tf_op jit(solution)/shard_map/ppermute | solution.py:241
  59.9 1.9 %collective-permute-start = (bf16[3,8,8192]{2,1,0:T(8,128)(2,1)S(1)}, bf16[3,8,8192]{2,1,0:T(8,128)(2,1)S(1)}, u32[]{:S(2)}, u32[]{:S(2)}) collective-permute-start(bf16[3,8,8192]{2,1,0:T(8,128)(2,1)S(1)} %get-tuple-element.13.own_ref), channel_id=1, source_target_pairs={{0,256},{64,320},{128,384},{192,448},{256,512},{320,576},{384,640}... | collective-permute-start | bytes 1179656 | tf_op jit(solution)/shard_map/ppermute | solution.py:241
  61.8 3.2 %all-to-all-done.1 = f32[24,1,128]{2,1,0:T(1,128)S(1)} async-done(((f32[24,1,128]{2,1,0:T(1,128)}), f32[24,1,128]{2,1,0:T(1,128)S(1)}, u32[]{:S(2)}, u32[]{:S(2)}) %all-to-all-start.1) | async-done | bytes 12320 | tf_op jit(solution)/shard_map/all_to_all | solution.py:219
  65.0 0.6 broadcast_in_dim.10
  65.6 10.2 %all-to-all-start.2 = ((f32[32,1,128]{2,1,0:T(1,128)}), f32[32,1,128]{2,1,0:T(1,128)S(1)}, u32[]{:S(2)}, u32[]{:S(2)}) async-start(f32[32,1,128]{2,1,0:T(1,128)} %broadcast_in_dim.10), calls=%async_computation.2 | async-start | bytes 32768 | tf_op jit(solution)/shard_map/all_to_all | solution.py:219
  75.9 1.0 dynamic-slice_bitcast_fusion.owned_ref
  77.6 6.8 %all-to-all-done.2.parts_ref = f32[32,1,128]{2,1,0:T(1,128)S(1)} async-done(((f32[32,1,128]{2,1,0:T(1,128)}), f32[32,1,128]{2,1,0:T(1,128)S(1)}, u32[]{:S(2)}, u32[]{:S(2)}) %all-to-all-start.2) | async-done | bytes 16416 | tf_op jit(solution)/shard_map/all_to_all | solution.py:219
  84.4 0.0 collective-permute-done.1.ahead_ref
  84.4 0.0 collective-permute-done.behind_ref
  84.4 1.1 shard_map.69
  85.5 0.0 copy-start
  85.5 22.1 %all_to_all.21.gathered_ref = bf16[4,3,8,8192]{3,2,1,0:T(8,128)(2,1)S(1)} all-to-all(bf16[4,3,8,8192]{3,2,1,0:T(8,128)(2,1)S(1)} %get-tuple-element.15), channel_id=1, replica_groups={{0,64,128,192},{256,320,384,448},{512,576,640,704},{1,65,129,193},{257,..., dimensions={0} | all-to-all | bytes 3145728 | tf_op jit(solution)/shard_map/all_to_all | solution.py:252
  107.6 0.0 copy-done
  107.6 1.9 %shard_map.70 = (bf16[12,8,8192]{2,1,0:T(8,128)(2,1)}, bf16[12,8,8192]{2,1,0:T(8,128)(2,1)}) custom-call(f32[8,128]{1,0:T(8,128)S(1)} %get-tuple-element.14.alpha_ref, bf16[4,3,8,8192]{3,2,1,0:T(8,128)(2,1)S(1)} %all_to_all.21.gathered_ref, bf16[12,8,8192]{2,1,0:T(8,128)(2,1)S(1)} %bitcast.12), custom_call_target="tpu_custom_call" | custom-call | tf_op jit(solution)/shard_map/pallas_call | solution.py:190
  (1 shorter events, 0.0 us)
Async XLA Ops:
  5.2 34.2 %copy-start.1 = (f32[8,8192]{1,0:T(8,128)S(1)}, f32[8,8192]{1,0:T(8,128)}, u32[]{:S(2)}) copy-start(f32[8,8192]{1,0:T(8,128)} %momentum_ref.3) | copy-start | bytes 786436
  40.2 24.7 %all-to-all-start.1 = ((f32[24,1,128]{2,1,0:T(1,128)}), f32[24,1,128]{2,1,0:T(1,128)S(1)}, u32[]{:S(2)}, u32[]{:S(2)}) async-start(f32[24,1,128]{2,1,0:T(1,128)} %get-tuple-element.11), calls=%async_computation.1 | async-start | bytes 24576 | tf_op jit(solution)/shard_map/all_to_all | solution.py:219
  55.2 29.2 %collective-permute-start.1 = (bf16[3,8,8192]{2,1,0:T(8,128)(2,1)S(1)}, bf16[3,8,8192]{2,1,0:T(8,128)(2,1)S(1)}, u32[]{:S(2)}, u32[]{:S(2)}) collective-permute-start(bf16[3,8,8192]{2,1,0:T(8,128)(2,1)S(1)} %get-tuple-element.13.own_ref), channel_id=1, source_target_pairs={{0,512},{64,576},{128,640},{192,704},{256,0},{320,64},{384,128},{4... | collective-permute-start | bytes 1179656 | tf_op jit(solution)/shard_map/ppermute | solution.py:241
  59.9 24.5 %collective-permute-start = (bf16[3,8,8192]{2,1,0:T(8,128)(2,1)S(1)}, bf16[3,8,8192]{2,1,0:T(8,128)(2,1)S(1)}, u32[]{:S(2)}, u32[]{:S(2)}) collective-permute-start(bf16[3,8,8192]{2,1,0:T(8,128)(2,1)S(1)} %get-tuple-element.13.own_ref), channel_id=1, source_target_pairs={{0,256},{64,320},{128,384},{192,448},{256,512},{320,576},{384,640}... | collective-permute-start | bytes 1179656 | tf_op jit(solution)/shard_map/ppermute | solution.py:241
  65.6 18.8 %all-to-all-start.2 = ((f32[32,1,128]{2,1,0:T(1,128)}), f32[32,1,128]{2,1,0:T(1,128)S(1)}, u32[]{:S(2)}, u32[]{:S(2)}) async-start(f32[32,1,128]{2,1,0:T(1,128)} %broadcast_in_dim.10), calls=%async_computation.2 | async-start | bytes 32768 | tf_op jit(solution)/shard_map/all_to_all | solution.py:219
  85.5 22.1 %copy-start = (bf16[1,96,8192]{2,1,0:T(8,128)(2,1)S(1)}, bf16[1,96,8192]{2,1,0:T(8,128)(2,1)}, u32[]{:S(2)}) copy-start(bf16[1,96,8192]{2,1,0:T(8,128)(2,1)} %param.5) | copy-start | bytes 4718596

commit v4 on v3

--- a/solution.py
+++ b/solution.py
@@ -33,7 +33,8 @@
         ]
 
     def put(i):
-        return pltpu.make_async_copy(decoded_tile.at[tile_rows(i)], decoded_ref.at[tile_rows(i)], sent.at[i])
+        slot = lax.rem(4 * (i // 2) + 3 * lax.rem(i, 2), 6)
+        return pltpu.make_async_copy(decoded_tile.at[tile_rows(i)], decoded_ref.at[tile_rows(slot)], sent.at[i])
 
     for i in range(count):
         for copy in fetch(i):
@@ -115,19 +116,17 @@
 
 
 def update_kernel(
-    entries, replicas, layer_ref, step_ref, parts_ref, average_ref, momentum_ref, own_ref, behind_ref, ahead_ref,
-    owned_ref, new_momentum_ref, copies_ref, alpha_ref,
+    entries, replicas, layer_ref, step_ref, parts_ref, own_ref, behind_ref, ahead_ref, owned_ref,
+    copies_ref, alpha_ref, factor_ref,
 ):
     steps = jnp.full(alpha_ref.shape, step_ref[0], jnp.int32).astype(jnp.float32)
     alpha_ref[...] = 0.9 / (1.0 + 0.1 * steps)
     squares = jnp.sum(jnp.sum(parts_ref[...], axis=0), keepdims=True)
     factor = 0.5 / jnp.sqrt(squares / entries + 1e-06)
     part = factor / replicas
+    factor_ref[...] = jnp.broadcast_to(factor, factor_ref.shape)
     layers = owned_ref.shape[0]
     step = 512
-    for start in range(0, average_ref.shape[1], step):
-        lanes = pl.ds(start, step)
-        new_momentum_ref[:, lanes] = 0.9 * momentum_ref[:, lanes] + factor * average_ref[:, lanes]
     for away, carried_ref in enumerate((own_ref, behind_ref, ahead_ref)):
         layer = lax.rem(layer_ref[0] + layers - away, layers)
         for start in range(0, own_ref.shape[2], step):
@@ -142,34 +141,40 @@
                 copies_ref[i, layer, :, lanes] = share
 
 
-def update(entries, replicas, layer, outer_step, parts, average, momentum, own, behind, ahead, owned, copies):
+def update(entries, replicas, layer, outer_step, parts, own, behind, ahead, owned, copies):
     layers, share, width = owned.shape
+    tile = jax.ShapeDtypeStruct((share, BLOCK), jnp.float32)
     return pl.pallas_call(
         functools.partial(update_kernel, entries, replicas),
-        out_shape=(
-            jax.ShapeDtypeStruct((share, width), jnp.float32),
-            jax.ShapeDtypeStruct((copies, layers, share, width), jnp.bfloat16),
-            jax.ShapeDtypeStruct((share, BLOCK), jnp.float32),
-        ),
-        in_specs=[pl.BlockSpec(memory_space=pltpu.SMEM)] * 2 + [WHOLE] * 7,
-        out_specs=(WHOLE, WHOLE, WHOLE),
+        out_shape=(jax.ShapeDtypeStruct((copies, layers, share, width), jnp.bfloat16), tile, tile),
+        in_specs=[pl.BlockSpec(memory_space=pltpu.SMEM)] * 2 + [WHOLE] * 5,
+        out_specs=(WHOLE,) * 3,
         compiler_params=VMEM,
-    )(layer, outer_step, parts, average, momentum, own, behind, ahead, owned)
-
-
-def mix_kernel(alpha_ref, gathered_ref, local_ref, new_global_ref, mixed_ref, mixed_tile, kept, sent):
+    )(layer, outer_step, parts, own, behind, ahead, owned)
+
+
+def mix_kernel(
+    order, alpha_ref, factor_ref, average_ref, momentum_ref, gathered_ref, local_ref,
+    new_global_ref, new_momentum_ref, mixed_ref, momentum_tile, mixed_tile, stored, kept, sent,
+):
     alpha = alpha_ref[:, 0:1]
     rest = 1.0 - alpha
+    factor = factor_ref[:, 0:1]
     columns, layers, _, width = gathered_ref.shape
     copies = []
     for layer in range(layers):
-        for i in range(columns):
-            j = layer * columns + i
+        for i, column in enumerate(order):
+            j = layer * columns + column
             copies.append(pltpu.make_async_copy(gathered_ref.at[i, layer], new_global_ref.at[j], kept.at[j]))
             copies[-1].start()
+    for start in range(0, width, 1024):
+        lanes = pl.ds(start, 1024)
+        momentum_tile[:, lanes] = 0.9 * momentum_ref[:, lanes] + factor * average_ref[:, lanes]
+    copies.append(pltpu.make_async_copy(momentum_tile, new_momentum_ref, stored))
+    copies[-1].start()
     for layer in range(layers):
-        for i in range(columns):
-            j = layer * columns + i
+        for i, column in enumerate(order):
+            j = layer * columns + column
             for start in range(0, width, 1024):
                 lanes = pl.ds(start, 1024)
                 mixed_tile[j, :, lanes] = (
@@ -182,23 +187,25 @@
         copy.wait()
 
 
-def mix(alpha, gathered, local_weights):
+def mix(order, alpha, factor, average, momentum, gathered, local_weights):
     columns, layers, share, width = gathered.shape
     count = layers * columns
     shape = jax.ShapeDtypeStruct((count, share, width), jnp.bfloat16)
     far = pl.BlockSpec(memory_space=pl.ANY)
     return pl.pallas_call(
-        mix_kernel,
-        out_shape=(shape, shape),
-        in_specs=[WHOLE, WHOLE, WHOLE],
-        out_specs=(far, far),
+        functools.partial(mix_kernel, order),
+        out_shape=(shape, jax.ShapeDtypeStruct(momentum.shape, jnp.float32), shape),
+        in_specs=[WHOLE] * 6,
+        out_specs=(far,) * 3,
         scratch_shapes=[
+            pltpu.VMEM(momentum.shape, jnp.float32),
             pltpu.VMEM(shape.shape, jnp.bfloat16),
+            pltpu.SemaphoreType.DMA(()),
             pltpu.SemaphoreType.DMA((count,)),
             pltpu.SemaphoreType.DMA((count,)),
         ],
         compiler_params=VMEM,
-    )(alpha, gathered, local_weights.reshape(shape.shape))
+    )(alpha, factor, average, momentum, gathered, local_weights.reshape(shape.shape))
 
 
 def grouped(lengths, inside):
@@ -233,8 +240,9 @@
     plane = grouped(lengths, ("x", "y"))
     line = grouped(lengths, ("z_lo", "z_hi", "core"))
     decoded = quantize(global_weights, local_weights[0])
+    slots = [(s % 3) * columns + (s % 2) * 2 + i for s in range(replicas // 2) for i in range(2)]
     parts = lax.all_to_all(
-        decoded.reshape(replicas, share, width), "rep", 0, 0, tiled=True
+        decoded.reshape(replicas, share, width), "rep", 0, 0, tiled=True, axis_index_groups=[slots]
     )
     average, carried, partial = totals(parts, outer_momentum, len(line[0]))
     behind, ahead = (
@@ -245,12 +253,15 @@
     partials = exchange(jnp.broadcast_to(partial[None], (len(plane[0]),) + partial.shape), plane)
     entries = float(rows_dev * peers * width)
     layer = (place // columns).astype(jnp.int32)[None]
-    new_momentum, copies, alpha = update(
-        entries, replicas, layer, outer_step, partials, average, outer_momentum, carried, behind, ahead, owned, columns
-    )
-    beside = [[i * columns + j for j in range(columns)] for i in range(layers)]
+    copies, alpha, factor = update(
+        entries, replicas, layer, outer_step, partials, carried, behind, ahead, owned, columns
+    )
+    order = (0, 1, 3, 2)
+    beside = [[i * columns + j for j in order] for i in range(layers)]
     gathered = lax.all_to_all(copies, "rep", 0, 0, tiled=True, axis_index_groups=beside)
-    new_global, mixed_local = mix(alpha, gathered, local_weights[0])
+    new_global, new_momentum, mixed_local = mix(
+        order, alpha, factor, average, outer_momentum, gathered, local_weights[0]
+    )
     return (
         new_global.reshape(rows_dev, width),
         new_momentum,

time: 110 us -> 109 us (level)
  starting transfers between devices: 31.8 us -> 30.7 us
where the time goes in v4:
time: 109 us; the launch traced here: 108 us
  blocking collectives  56.7 us (52%)
  starting transfers between devices  30.7 us (28%)
  waiting for transfers between devices  10 us (9%)
  Pallas kernels  7.87 us (7%)
  local copies, waits for them, and re-layouts  1.66 us (2%)
  between operations  1.38 us (1%)
    all_to_all x1, blocking collectives, shards(): lax.all_to_all(decoded.reshape(replicas, share, width), 'rep', 0, 0, tile...  34.6 us
    all_to_all x2, starting transfers between devices, exchange(): lax.all_to_all(copies, ('rep', 'fsdp'), 0, 0, tiled=True, axis_index_grou...  24.1 us
    all_to_all x1, blocking collectives, shards(): lax.all_to_all(copies, 'rep', 0, 0, tiled=True, axis_index_groups=beside)  22.1 us
    all_to_all x2, waiting for transfers between devices, exchange(): lax.all_to_all(copies, ('rep', 'fsdp'), 0, 0, tiled=True, axis_index_grou...  9.99 us
    ppermute x2, starting transfers between devices, shards(): lax.ppermute(carried, 'rep', [(i, (i + away * columns) % replicas) for i...  6.58 us
    pallas_call x1, Pallas kernels, quantize(): pl.pallas_call(quantize_kernel, out_shape=jax.ShapeDtypeStruct(shape, jnp...  4.58 us
  transfers between devices with their start and end apart: 4, of which 2 were waited for; matrix products, arithmetic and copies ran while one was open for 2% of the time, Pallas kernels for 0%

profile of v4, /device:TPU:2, one launch (start us, length us, event | category | flops | bytes accessed | tf_op | source)
XLA Modules:
  0.0 108.3 jit_solution(10957017776480293573)
XLA Ops:
  0.6 4.6 %shard_map.67 = bf16[96,8192]{1,0:T(8,128)(2,1)} custom-call(bf16[96,8192]{1,0:T(8,128)(2,1)} %global_ref.1, bf16[96,8192]{1,0:T(8,128)(2,1)} %bitcast.11), custom_call_target="tpu_custom_call" | custom-call | tf_op jit(solution)/shard_map/pallas_call | solution.py:68
  5.2 0.0 copy-start.1
  5.2 34.6 %all_to_all.20.parts_ref = bf16[12,8,8192]{2,1,0:T(8,128)(2,1)S(1)} all-to-all(bf16[12,8,8192]{2,1,0:T(8,128)(2,1)} %bitcast.13), channel_id=1, replica_groups={{0,64,384,448,512,576,128,192,256,320,640,704},{1,65,385,449,513,577,12..., dimensions={0} | all-to-all | bytes 3145728 | tf_op jit(solution)/shard_map/all_to_all | solution.py:244
  39.8 0.0 copy-done.1
  39.8 0.8 shard_map.68
  40.6 14.8 %all-to-all-start.1 = ((f32[24,1,128]{2,1,0:T(1,128)}), f32[24,1,128]{2,1,0:T(1,128)S(1)}, u32[]{:S(2)}, u32[]{:S(2)}) async-start(f32[24,1,128]{2,1,0:T(1,128)} %get-tuple-element.12), calls=%async_computation.1 | async-start | bytes 24576 | tf_op jit(solution)/shard_map/all_to_all | solution.py:226
  55.4 4.7 %collective-permute-start.1 = (bf16[3,8,8192]{2,1,0:T(8,128)(2,1)S(1)}, bf16[3,8,8192]{2,1,0:T(8,128)(2,1)S(1)}, u32[]{:S(2)}, u32[]{:S(2)}) collective-permute-start(bf16[3,8,8192]{2,1,0:T(8,128)(2,1)S(1)} %get-tuple-element.13.own_ref), channel_id=1, source_target_pairs={{0,512},{64,576},{128,640},{192,704},{256,0},{320,64},{384,128},{4... | collective-permute-start | bytes 1179656 | tf_op jit(solution)/shard_map/ppermute | solution.py:249
  60.1 1.9 %collective-permute-start = (bf16[3,8,8192]{2,1,0:T(8,128)(2,1)S(1)}, bf16[3,8,8192]{2,1,0:T(8,128)(2,1)S(1)}, u32[]{:S(2)}, u32[]{:S(2)}) collective-permute-start(bf16[3,8,8192]{2,1,0:T(8,128)(2,1)S(1)} %get-tuple-element.13.own_ref), channel_id=1, source_target_pairs={{0,256},{64,320},{128,384},{192,448},{256,512},{320,576},{384,640}... | collective-permute-start | bytes 1179656 | tf_op jit(solution)/shard_map/ppermute | solution.py:249
  62.0 3.2 %all-to-all-done.1 = f32[24,1,128]{2,1,0:T(1,128)S(1)} async-done(((f32[24,1,128]{2,1,0:T(1,128)}), f32[24,1,128]{2,1,0:T(1,128)S(1)}, u32[]{:S(2)}, u32[]{:S(2)}) %all-to-all-start.1) | async-done | bytes 12320 | tf_op jit(solution)/shard_map/all_to_all | solution.py:226
  65.2 0.6 broadcast_in_dim.10
  65.8 9.3 %all-to-all-start.2 = ((f32[32,1,128]{2,1,0:T(1,128)}), f32[32,1,128]{2,1,0:T(1,128)S(1)}, u32[]{:S(2)}, u32[]{:S(2)}) async-start(f32[32,1,128]{2,1,0:T(1,128)} %broadcast_in_dim.10), calls=%async_computation.2 | async-start | bytes 32768 | tf_op jit(solution)/shard_map/all_to_all | solution.py:226
  75.2 1.0 dynamic-slice_bitcast_fusion.owned_ref
  76.9 6.8 %all-to-all-done.2.parts_ref = f32[32,1,128]{2,1,0:T(1,128)S(1)} async-done(((f32[32,1,128]{2,1,0:T(1,128)}), f32[32,1,128]{2,1,0:T(1,128)S(1)}, u32[]{:S(2)}, u32[]{:S(2)}) %all-to-all-start.2) | async-done | bytes 16416 | tf_op jit(solution)/shard_map/all_to_all | solution.py:226
  83.7 0.0 collective-permute-done.1.ahead_ref
  83.7 0.0 collective-permute-done.behind_ref
  83.7 0.5 shard_map.69
  84.2 0.0 copy-start
  84.2 22.1 %all_to_all.21.gathered_ref = bf16[4,3,8,8192]{3,2,1,0:T(8,128)(2,1)S(1)} all-to-all(bf16[4,3,8,8192]{3,2,1,0:T(8,128)(2,1)S(1)} %get-tuple-element.17), channel_id=1, replica_groups={{0,64,192,128},{256,320,448,384},{512,576,704,640},{1,65,193,129},{257,..., dimensions={0} | all-to-all | bytes 3145728 | tf_op jit(solution)/shard_map/all_to_all | solution.py:261
  106.3 0.0 copy-done
  106.3 2.0 %shard_map.70 = (bf16[12,8,8192]{2,1,0:T(8,128)(2,1)}, f32[8,8192]{1,0:T(8,128)}, bf16[12,8,8192]{2,1,0:T(8,128)(2,1)}) custom-call(f32[8,128]{1,0:T(8,128)S(1)} %get-tuple-element.14.alpha_ref, f32[8,128]{1,0:T(8,128)S(1)} %get-tuple-element.15.factor_ref, f32[8,8192]{1,0:T(8,128)S(1)} %get-tuple-element.16.average_ref, f32[8,8192]{1,0:T(8,128)S(1)} %copy-done.1, ...), custom_call_target="tpu_custom_call" | custom-call | tf_op jit(solution)/shard_map/pallas_call | solution.py:195
  (1 shorter events, 0.0 us)
Async XLA Ops:
  5.2 34.6 %copy-start.1 = (f32[8,8192]{1,0:T(8,128)S(1)}, f32[8,8192]{1,0:T(8,128)}, u32[]{:S(2)}) copy-start(f32[8,8192]{1,0:T(8,128)} %momentum_ref.3) | copy-start | bytes 786436
  40.6 24.5 %all-to-all-start.1 = ((f32[24,1,128]{2,1,0:T(1,128)}), f32[24,1,128]{2,1,0:T(1,128)S(1)}, u32[]{:S(2)}, u32[]{:S(2)}) async-start(f32[24,1,128]{2,1,0:T(1,128)} %get-tuple-element.12), calls=%async_computation.1 | async-start | bytes 24576 | tf_op jit(solution)/shard_map/all_to_all | solution.py:226
  55.4 28.3 %collective-permute-start.1 = (bf16[3,8,8192]{2,1,0:T(8,128)(2,1)S(1)}, bf16[3,8,8192]{2,1,0:T(8,128)(2,1)S(1)}, u32[]{:S(2)}, u32[]{:S(2)}) collective-permute-start(bf16[3,8,8192]{2,1,0:T(8,128)(2,1)S(1)} %get-tuple-element.13.own_ref), channel_id=1, source_target_pairs={{0,512},{64,576},{128,640},{192,704},{256,0},{320,64},{384,128},{4... | collective-permute-start | bytes 1179656 | tf_op jit(solution)/shard_map/ppermute | solution.py:249
  60.1 23.6 %collective-permute-start = (bf16[3,8,8192]{2,1,0:T(8,128)(2,1)S(1)}, bf16[3,8,8192]{2,1,0:T(8,128)(2,1)S(1)}, u32[]{:S(2)}, u32[]{:S(2)}) collective-permute-start(bf16[3,8,8192]{2,1,0:T(8,128)(2,1)S(1)} %get-tuple-element.13.own_ref), channel_id=1, source_target_pairs={{0,256},{64,320},{128,384},{192,448},{256,512},{320,576},{384,640}... | collective-permute-start | bytes 1179656 | tf_op jit(solution)/shard_map/ppermute | solution.py:249
  65.8 17.9 %all-to-all-start.2 = ((f32[32,1,128]{2,1,0:T(1,128)}), f32[32,1,128]{2,1,0:T(1,128)S(1)}, u32[]{:S(2)}, u32[]{:S(2)}) async-start(f32[32,1,128]{2,1,0:T(1,128)} %broadcast_in_dim.10), calls=%async_computation.2 | async-start | bytes 32768 | tf_op jit(solution)/shard_map/all_to_all | solution.py:226
  84.2 22.1 %copy-start = (bf16[1,96,8192]{2,1,0:T(8,128)(2,1)S(1)}, bf16[1,96,8192]{2,1,0:T(8,128)(2,1)}, u32[]{:S(2)}) copy-start(bf16[1,96,8192]{2,1,0:T(8,128)(2,1)} %param.5) | copy-start | bytes 4718596

commit v5 on v4

--- a/solution.py
+++ b/solution.py
@@ -10,6 +10,7 @@
 
 BLOCK = 128
 SPLIT = 2.0**23 + 1.0
+TILES = (3, 5, 2, 0, 4, 1)
 VMEM = pltpu.CompilerParams(vmem_limit_bytes=24 * 2**20)
 WHOLE = pl.BlockSpec(memory_space=pltpu.VMEM)
 
@@ -33,7 +34,7 @@
         ]
 
     def put(i):
-        slot = lax.rem(4 * (i // 2) + 3 * lax.rem(i, 2), 6)
+        slot = sum(jnp.where(i == tile, s, 0) for s, tile in enumerate(TILES))
         return pltpu.make_async_copy(decoded_tile.at[tile_rows(i)], decoded_ref.at[tile_rows(slot)], sent.at[i])
 
     for i in range(count):
@@ -49,8 +50,7 @@
             delta = global_tile[at].astype(jnp.float32) - local_tile[at].astype(jnp.float32)
             magnitude = jnp.abs(delta)
             largest = jnp.maximum(jnp.max(magnitude, axis=1, keepdims=True), 2.0**-24)
-            near = one_bit(largest)
-            scale = jnp.minimum(jnp.where(near >= largest, near, near + near), 2.0**15)
+            scale = jnp.minimum(one_bit(largest * (1.5 - 2.0**-23)), 2.0**15)
             least = scale * 2.0**-7
             level = jnp.maximum(one_bit(magnitude), least + least)
             level = jnp.where(magnitude >= least, level, 0.0)
@@ -240,7 +240,7 @@
     plane = grouped(lengths, ("x", "y"))
     line = grouped(lengths, ("z_lo", "z_hi", "core"))
     decoded = quantize(global_weights, local_weights[0])
-    slots = [(s % 3) * columns + (s % 2) * 2 + i for s in range(replicas // 2) for i in range(2)]
+    slots = [2 * tile + i for tile in TILES for i in range(2)]
     parts = lax.all_to_all(
         decoded.reshape(replicas, share, width), "rep", 0, 0, tiled=True, axis_index_groups=[slots]
     )

time: 109 us -> 108 us (level)
  blocking collectives: 56.7 us -> 55.2 us
    all_to_all x1, blocking collectives: 34.6 us -> 33.1 us  [shards(): lax.all_to_all(decoded.reshape(replicas, share, width), 'rep', 0, 0, tile...]
where the time goes in v5:
time: 108 us; the launch traced here: 107 us
  blocking collectives  55.2 us (51%)
  starting transfers between devices  31.5 us (29%)
  waiting for transfers between devices  10 us (9%)
  Pallas kernels  7.54 us (7%)
  local copies, waits for them, and re-layouts  1.66 us (2%)
  between operations  1.38 us (1%)
    all_to_all x1, blocking collectives, shards(): lax.all_to_all(decoded.reshape(replicas, share, width), 'rep', 0, 0, tile...  33.1 us
    all_to_all x2, starting transfers between devices, exchange(): lax.all_to_all(copies, ('rep', 'fsdp'), 0, 0, tiled=True, axis_index_grou...  24.9 us
    all_to_all x1, blocking collectives, shards(): lax.all_to_all(copies, 'rep', 0, 0, tiled=True, axis_index_groups=beside)  22.1 us
    all_to_all x2, waiting for transfers between devices, exchange(): lax.all_to_all(copies, ('rep', 'fsdp'), 0, 0, tiled=True, axis_index_grou...  9.99 us
    ppermute x2, starting transfers between devices, shards(): lax.ppermute(carried, 'rep', [(i, (i + away * columns) % replicas) for i...  6.58 us
    pallas_call x1, Pallas kernels, quantize(): pl.pallas_call(quantize_kernel, out_shape=jax.ShapeDtypeStruct(shape, jnp...  4.25 us
  transfers between devices with their start and end apart: 4, of which 2 were waited for; matrix products, arithmetic and copies ran while one was open for 2% of the time, Pallas kernels for 0%

profile of v5, /device:TPU:2, one launch (start us, length us, event | category | flops | bytes accessed | tf_op | source)
XLA Modules:
  0.0 107.3 jit_solution(7337059634471525240)
XLA Ops:
  0.6 4.3 %shard_map.67 = bf16[96,8192]{1,0:T(8,128)(2,1)} custom-call(bf16[96,8192]{1,0:T(8,128)(2,1)} %global_ref.1, bf16[96,8192]{1,0:T(8,128)(2,1)} %bitcast.11), custom_call_target="tpu_custom_call" | custom-call | tf_op jit(solution)/shard_map/pallas_call | solution.py:68
  4.9 0.0 copy-start.1
  4.9 33.1 %all_to_all.20.parts_ref = bf16[12,8,8192]{2,1,0:T(8,128)(2,1)S(1)} all-to-all(bf16[12,8,8192]{2,1,0:T(8,128)(2,1)} %bitcast.13), channel_id=1, replica_groups={{384,448,640,704,256,320,0,64,512,576,128,192},{385,449,641,705,257,321..., dimensions={0} | all-to-all | bytes 3145728 | tf_op jit(solution)/shard_map/all_to_all | solution.py:244
  38.0 0.0 copy-done.1
  38.0 0.8 shard_map.68
  38.8 15.0 %all-to-all-start.1 = ((f32[24,1,128]{2,1,0:T(1,128)}), f32[24,1,128]{2,1,0:T(1,128)S(1)}, u32[]{:S(2)}, u32[]{:S(2)}) async-start(f32[24,1,128]{2,1,0:T(1,128)} %get-tuple-element.12), calls=%async_computation.1 | async-start | bytes 24576 | tf_op jit(solution)/shard_map/all_to_all | solution.py:226
  53.9 4.7 %collective-permute-start.1 = (bf16[3,8,8192]{2,1,0:T(8,128)(2,1)S(1)}, bf16[3,8,8192]{2,1,0:T(8,128)(2,1)S(1)}, u32[]{:S(2)}, u32[]{:S(2)}) collective-permute-start(bf16[3,8,8192]{2,1,0:T(8,128)(2,1)S(1)} %get-tuple-element.13.own_ref), channel_id=1, source_target_pairs={{0,512},{64,576},{128,640},{192,704},{256,0},{320,64},{384,128},{4... | collective-permute-start | bytes 1179656 | tf_op jit(solution)/shard_map/ppermute | solution.py:249
  58.5 1.9 %collective-permute-start = (bf16[3,8,8192]{2,1,0:T(8,128)(2,1)S(1)}, bf16[3,8,8192]{2,1,0:T(8,128)(2,1)S(1)}, u32[]{:S(2)}, u32[]{:S(2)}) collective-permute-start(bf16[3,8,8192]{2,1,0:T(8,128)(2,1)S(1)} %get-tuple-element.13.own_ref), channel_id=1, source_target_pairs={{0,256},{64,320},{128,384},{192,448},{256,512},{320,576},{384,640}... | collective-permute-start | bytes 1179656 | tf_op jit(solution)/shard_map/ppermute | solution.py:249
  60.5 3.2 %all-to-all-done.1 = f32[24,1,128]{2,1,0:T(1,128)S(1)} async-done(((f32[24,1,128]{2,1,0:T(1,128)}), f32[24,1,128]{2,1,0:T(1,128)S(1)}, u32[]{:S(2)}, u32[]{:S(2)}) %all-to-all-start.1) | async-done | bytes 12320 | tf_op jit(solution)/shard_map/all_to_all | solution.py:226
  63.7 0.6 broadcast_in_dim.10
  64.3 9.9 %all-to-all-start.2 = ((f32[32,1,128]{2,1,0:T(1,128)}), f32[32,1,128]{2,1,0:T(1,128)S(1)}, u32[]{:S(2)}, u32[]{:S(2)}) async-start(f32[32,1,128]{2,1,0:T(1,128)} %broadcast_in_dim.10), calls=%async_computation.2 | async-start | bytes 32768 | tf_op jit(solution)/shard_map/all_to_all | solution.py:226
  74.1 1.0 dynamic-slice_bitcast_fusion.owned_ref
  75.8 6.8 %all-to-all-done.2.parts_ref = f32[32,1,128]{2,1,0:T(1,128)S(1)} async-done(((f32[32,1,128]{2,1,0:T(1,128)}), f32[32,1,128]{2,1,0:T(1,128)S(1)}, u32[]{:S(2)}, u32[]{:S(2)}) %all-to-all-start.2) | async-done | bytes 16416 | tf_op jit(solution)/shard_map/all_to_all | solution.py:226
  82.7 0.0 collective-permute-done.1.ahead_ref
  82.7 0.0 collective-permute-done.behind_ref
  82.7 0.5 shard_map.69
  83.2 0.0 copy-start
  83.2 22.1 %all_to_all.21.gathered_ref = bf16[4,3,8,8192]{3,2,1,0:T(8,128)(2,1)S(1)} all-to-all(bf16[4,3,8,8192]{3,2,1,0:T(8,128)(2,1)S(1)} %get-tuple-element.17), channel_id=1, replica_groups={{0,64,192,128},{256,320,448,384},{512,576,704,640},{1,65,193,129},{257,..., dimensions={0} | all-to-all | bytes 3145728 | tf_op jit(solution)/shard_map/all_to_all | solution.py:261
  105.3 0.0 copy-done
  105.3 2.0 %shard_map.70 = (bf16[12,8,8192]{2,1,0:T(8,128)(2,1)}, f32[8,8192]{1,0:T(8,128)}, bf16[12,8,8192]{2,1,0:T(8,128)(2,1)}) custom-call(f32[8,128]{1,0:T(8,128)S(1)} %get-tuple-element.14.alpha_ref, f32[8,128]{1,0:T(8,128)S(1)} %get-tuple-element.15.factor_ref, f32[8,8192]{1,0:T(8,128)S(1)} %get-tuple-element.16.average_ref, f32[8,8192]{1,0:T(8,128)S(1)} %copy-done.1, ...), custom_call_target="tpu_custom_call" | custom-call | tf_op jit(solution)/shard_map/pallas_call | solution.py:195
  (1 shorter events, 0.0 us)
Async XLA Ops:
  4.9 33.1 %copy-start.1 = (f32[8,8192]{1,0:T(8,128)S(1)}, f32[8,8192]{1,0:T(8,128)}, u32[]{:S(2)}) copy-start(f32[8,8192]{1,0:T(8,128)} %momentum_ref.3) | copy-start | bytes 786436
  38.8 24.8 %all-to-all-start.1 = ((f32[24,1,128]{2,1,0:T(1,128)}), f32[24,1,128]{2,1,0:T(1,128)S(1)}, u32[]{:S(2)}, u32[]{:S(2)}) async-start(f32[24,1,128]{2,1,0:T(1,128)} %get-tuple-element.12), calls=%async_computation.1 | async-start | bytes 24576 | tf_op jit(solution)/shard_map/all_to_all | solution.py:226
  53.9 28.8 %collective-permute-start.1 = (bf16[3,8,8192]{2,1,0:T(8,128)(2,1)S(1)}, bf16[3,8,8192]{2,1,0:T(8,128)(2,1)S(1)}, u32[]{:S(2)}, u32[]{:S(2)}) collective-permute-start(bf16[3,8,8192]{2,1,0:T(8,128)(2,1)S(1)} %get-tuple-element.13.own_ref), channel_id=1, source_target_pairs={{0,512},{64,576},{128,640},{192,704},{256,0},{320,64},{384,128},{4... | collective-permute-start | bytes 1179656 | tf_op jit(solution)/shard_map/ppermute | solution.py:249
  58.5 24.2 %collective-permute-start = (bf16[3,8,8192]{2,1,0:T(8,128)(2,1)S(1)}, bf16[3,8,8192]{2,1,0:T(8,128)(2,1)S(1)}, u32[]{:S(2)}, u32[]{:S(2)}) collective-permute-start(bf16[3,8,8192]{2,1,0:T(8,128)(2,1)S(1)} %get-tuple-element.13.own_ref), channel_id=1, source_target_pairs={{0,256},{64,320},{128,384},{192,448},{256,512},{320,576},{384,640}... | collective-permute-start | bytes 1179656 | tf_op jit(solution)/shard_map/ppermute | solution.py:249
  64.3 18.4 %all-to-all-start.2 = ((f32[32,1,128]{2,1,0:T(1,128)}), f32[32,1,128]{2,1,0:T(1,128)S(1)}, u32[]{:S(2)}, u32[]{:S(2)}) async-start(f32[32,1,128]{2,1,0:T(1,128)} %broadcast_in_dim.10), calls=%async_computation.2 | async-start | bytes 32768 | tf_op jit(solution)/shard_map/all_to_all | solution.py:226
  83.2 22.1 %copy-start = (bf16[1,96,8192]{2,1,0:T(8,128)(2,1)S(1)}, bf16[1,96,8192]{2,1,0:T(8,128)(2,1)}, u32[]{:S(2)}) copy-start(bf16[1,96,8192]{2,1,0:T(8,128)(2,1)} %param.5) | copy-start | bytes 4718596

commit v6 on v5

--- a/solution.py
+++ b/solution.py
@@ -10,7 +10,7 @@
 
 BLOCK = 128
 SPLIT = 2.0**23 + 1.0
-TILES = (3, 5, 2, 0, 4, 1)
+TILES = (2, 0, 5, 4, 1, 3)
 VMEM = pltpu.CompilerParams(vmem_limit_bytes=24 * 2**20)
 WHOLE = pl.BlockSpec(memory_space=pltpu.VMEM)
 

time: 108 us -> 107 us (level)
  no operation moved by 1% of the time
where the time goes in v6:
time: 107 us
  blocking collectives  55.4 us (52%)
  starting transfers between devices  30.8 us (29%)
  waiting for transfers between devices  10 us (9%)
  Pallas kernels  7.54 us (7%)
  local copies, waits for them, and re-layouts  1.66 us (2%)
  between operations  1.38 us (1%)
    all_to_all x1, blocking collectives, shards(): lax.all_to_all(decoded.reshape(replicas, share, width), 'rep', 0, 0, tile...  33.3 us
    all_to_all x2, starting transfers between devices, exchange(): lax.all_to_all(copies, ('rep', 'fsdp'), 0, 0, tiled=True, axis_index_grou...  24.2 us
    all_to_all x1, blocking collectives, shards(): lax.all_to_all(copies, 'rep', 0, 0, tiled=True, axis_index_groups=beside)  22.1 us
    all_to_all x2, waiting for transfers between devices, exchange(): lax.all_to_all(copies, ('rep', 'fsdp'), 0, 0, tiled=True, axis_index_grou...  9.99 us
    ppermute x2, starting transfers between devices, shards(): lax.ppermute(carried, 'rep', [(i, (i + away * columns) % replicas) for i...  6.58 us
    pallas_call x1, Pallas kernels, quantize(): pl.pallas_call(quantize_kernel, out_shape=jax.ShapeDtypeStruct(shape, jnp...  4.25 us
  transfers between devices with their start and end apart: 4, of which 2 were waited for; matrix products, arithmetic and copies ran while one was open for 2% of the time, Pallas kernels for 0%

profile of v6, /device:TPU:2, one launch (start us, length us, event | category | flops | bytes accessed | tf_op | source)
XLA Modules:
  0.0 106.8 jit_solution(361836524843937342)
XLA Ops:
  0.6 4.3 %shard_map.67 = bf16[96,8192]{1,0:T(8,128)(2,1)} custom-call(bf16[96,8192]{1,0:T(8,128)(2,1)} %global_ref.1, bf16[96,8192]{1,0:T(8,128)(2,1)} %bitcast.11), custom_call_target="tpu_custom_call" | custom-call | tf_op jit(solution)/shard_map/pallas_call | solution.py:68
  4.9 0.0 copy-start.1
  4.9 33.3 %all_to_all.20.parts_ref = bf16[12,8,8192]{2,1,0:T(8,128)(2,1)S(1)} all-to-all(bf16[12,8,8192]{2,1,0:T(8,128)(2,1)} %bitcast.13), channel_id=1, replica_groups={{256,320,0,64,640,704,512,576,128,192,384,448},{257,321,1,65,641,705,51..., dimensions={0} | all-to-all | bytes 3145728 | tf_op jit(solution)/shard_map/all_to_all | solution.py:244
  38.2 0.0 copy-done.1
  38.2 0.8 shard_map.68
  39.0 14.5 %all-to-all-start.1 = ((f32[24,1,128]{2,1,0:T(1,128)}), f32[24,1,128]{2,1,0:T(1,128)S(1)}, u32[]{:S(2)}, u32[]{:S(2)}) async-start(f32[24,1,128]{2,1,0:T(1,128)} %get-tuple-element.12), calls=%async_computation.1 | async-start | bytes 24576 | tf_op jit(solution)/shard_map/all_to_all | solution.py:226
  53.6 4.7 %collective-permute-start.1 = (bf16[3,8,8192]{2,1,0:T(8,128)(2,1)S(1)}, bf16[3,8,8192]{2,1,0:T(8,128)(2,1)S(1)}, u32[]{:S(2)}, u32[]{:S(2)}) collective-permute-start(bf16[3,8,8192]{2,1,0:T(8,128)(2,1)S(1)} %get-tuple-element.13.own_ref), channel_id=1, source_target_pairs={{0,512},{64,576},{128,640},{192,704},{256,0},{320,64},{384,128},{4... | collective-permute-start | bytes 1179656 | tf_op jit(solution)/shard_map/ppermute | solution.py:249
  58.2 1.9 %collective-permute-start = (bf16[3,8,8192]{2,1,0:T(8,128)(2,1)S(1)}, bf16[3,8,8192]{2,1,0:T(8,128)(2,1)S(1)}, u32[]{:S(2)}, u32[]{:S(2)}) collective-permute-start(bf16[3,8,8192]{2,1,0:T(8,128)(2,1)S(1)} %get-tuple-element.13.own_ref), channel_id=1, source_target_pairs={{0,256},{64,320},{128,384},{192,448},{256,512},{320,576},{384,640}... | collective-permute-start | bytes 1179656 | tf_op jit(solution)/shard_map/ppermute | solution.py:249
  60.2 3.2 %all-to-all-done.1 = f32[24,1,128]{2,1,0:T(1,128)S(1)} async-done(((f32[24,1,128]{2,1,0:T(1,128)}), f32[24,1,128]{2,1,0:T(1,128)S(1)}, u32[]{:S(2)}, u32[]{:S(2)}) %all-to-all-start.1) | async-done | bytes 12320 | tf_op jit(solution)/shard_map/all_to_all | solution.py:226
  63.4 0.6 broadcast_in_dim.10
  64.0 9.7 %all-to-all-start.2 = ((f32[32,1,128]{2,1,0:T(1,128)}), f32[32,1,128]{2,1,0:T(1,128)S(1)}, u32[]{:S(2)}, u32[]{:S(2)}) async-start(f32[32,1,128]{2,1,0:T(1,128)} %broadcast_in_dim.10), calls=%async_computation.2 | async-start | bytes 32768 | tf_op jit(solution)/shard_map/all_to_all | solution.py:226
  73.7 1.0 dynamic-slice_bitcast_fusion.owned_ref
  75.4 6.8 %all-to-all-done.2.parts_ref = f32[32,1,128]{2,1,0:T(1,128)S(1)} async-done(((f32[32,1,128]{2,1,0:T(1,128)}), f32[32,1,128]{2,1,0:T(1,128)S(1)}, u32[]{:S(2)}, u32[]{:S(2)}) %all-to-all-start.2) | async-done | bytes 16416 | tf_op jit(solution)/shard_map/all_to_all | solution.py:226
  82.2 0.0 collective-permute-done.1.ahead_ref
  82.2 0.0 collective-permute-done.behind_ref
  82.2 0.5 shard_map.69
  82.7 0.0 copy-start
  82.7 22.1 %all_to_all.21.gathered_ref = bf16[4,3,8,8192]{3,2,1,0:T(8,128)(2,1)S(1)} all-to-all(bf16[4,3,8,8192]{3,2,1,0:T(8,128)(2,1)S(1)} %get-tuple-element.17), channel_id=1, replica_groups={{0,64,192,128},{256,320,448,384},{512,576,704,640},{1,65,193,129},{257,..., dimensions={0} | all-to-all | bytes 3145728 | tf_op jit(solution)/shard_map/all_to_all | solution.py:261
  104.8 0.0 copy-done
  104.8 2.0 %shard_map.70 = (bf16[12,8,8192]{2,1,0:T(8,128)(2,1)}, f32[8,8192]{1,0:T(8,128)}, bf16[12,8,8192]{2,1,0:T(8,128)(2,1)}) custom-call(f32[8,128]{1,0:T(8,128)S(1)} %get-tuple-element.14.alpha_ref, f32[8,128]{1,0:T(8,128)S(1)} %get-tuple-element.15.factor_ref, f32[8,8192]{1,0:T(8,128)S(1)} %get-tuple-element.16.average_ref, f32[8,8192]{1,0:T(8,128)S(1)} %copy-done.1, ...), custom_call_target="tpu_custom_call" | custom-call | tf_op jit(solution)/shard_map/pallas_call | solution.py:195
  (1 shorter events, 0.0 us)
Async XLA Ops:
  4.9 33.3 %copy-start.1 = (f32[8,8192]{1,0:T(8,128)S(1)}, f32[8,8192]{1,0:T(8,128)}, u32[]{:S(2)}) copy-start(f32[8,8192]{1,0:T(8,128)} %momentum_ref.3) | copy-start | bytes 786436
  39.0 24.3 %all-to-all-start.1 = ((f32[24,1,128]{2,1,0:T(1,128)}), f32[24,1,128]{2,1,0:T(1,128)S(1)}, u32[]{:S(2)}, u32[]{:S(2)}) async-start(f32[24,1,128]{2,1,0:T(1,128)} %get-tuple-element.12), calls=%async_computation.1 | async-start | bytes 24576 | tf_op jit(solution)/shard_map/all_to_all | solution.py:226
  53.6 28.7 %collective-permute-start.1 = (bf16[3,8,8192]{2,1,0:T(8,128)(2,1)S(1)}, bf16[3,8,8192]{2,1,0:T(8,128)(2,1)S(1)}, u32[]{:S(2)}, u32[]{:S(2)}) collective-permute-start(bf16[3,8,8192]{2,1,0:T(8,128)(2,1)S(1)} %get-tuple-element.13.own_ref), channel_id=1, source_target_pairs={{0,512},{64,576},{128,640},{192,704},{256,0},{320,64},{384,128},{4... | collective-permute-start | bytes 1179656 | tf_op jit(solution)/shard_map/ppermute | solution.py:249
  58.2 24.0 %collective-permute-start = (bf16[3,8,8192]{2,1,0:T(8,128)(2,1)S(1)}, bf16[3,8,8192]{2,1,0:T(8,128)(2,1)S(1)}, u32[]{:S(2)}, u32[]{:S(2)}) collective-permute-start(bf16[3,8,8192]{2,1,0:T(8,128)(2,1)S(1)} %get-tuple-element.13.own_ref), channel_id=1, source_target_pairs={{0,256},{64,320},{128,384},{192,448},{256,512},{320,576},{384,640}... | collective-permute-start | bytes 1179656 | tf_op jit(solution)/shard_map/ppermute | solution.py:249
  64.0 18.2 %all-to-all-start.2 = ((f32[32,1,128]{2,1,0:T(1,128)}), f32[32,1,128]{2,1,0:T(1,128)S(1)}, u32[]{:S(2)}, u32[]{:S(2)}) async-start(f32[32,1,128]{2,1,0:T(1,128)} %broadcast_in_dim.10), calls=%async_computation.2 | async-start | bytes 32768 | tf_op jit(solution)/shard_map/all_to_all | solution.py:226
  82.7 22.1 %copy-start = (bf16[1,96,8192]{2,1,0:T(8,128)(2,1)S(1)}, bf16[1,96,8192]{2,1,0:T(8,128)(2,1)}, u32[]{:S(2)}) copy-start(bf16[1,96,8192]{2,1,0:T(8,128)(2,1)} %param.5) | copy-start | bytes 4718596

commit v7 on v6

--- a/solution.py
+++ b/solution.py
@@ -10,7 +10,7 @@
 
 BLOCK = 128
 SPLIT = 2.0**23 + 1.0
-TILES = (2, 0, 5, 4, 1, 3)
+TILES = (2, 0, 1, 5, 4, 3)
 VMEM = pltpu.CompilerParams(vmem_limit_bytes=24 * 2**20)
 WHOLE = pl.BlockSpec(memory_space=pltpu.VMEM)
 

time: 107 us -> 107 us (level)
  no operation moved by 1% of the time
where the time goes in v7:
time: 107 us; the launch traced here: 106 us
  blocking collectives  55.2 us (52%)
  starting transfers between devices  30.5 us (29%)
  waiting for transfers between devices  10 us (9%)
  Pallas kernels  7.54 us (7%)
  local copies, waits for them, and re-layouts  1.66 us (2%)
  between operations  1.38 us (1%)
    all_to_all x1, blocking collectives, shards(): lax.all_to_all(decoded.reshape(replicas, share, width), 'rep', 0, 0, tile...  33.1 us
    all_to_all x2, starting transfers between devices, exchange(): lax.all_to_all(copies, ('rep', 'fsdp'), 0, 0, tiled=True, axis_index_grou...  23.9 us
    all_to_all x1, blocking collectives, shards(): lax.all_to_all(copies, 'rep', 0, 0, tiled=True, axis_index_groups=beside)  22.1 us
    all_to_all x2, waiting for transfers between devices, exchange(): lax.all_to_all(copies, ('rep', 'fsdp'), 0, 0, tiled=True, axis_index_grou...  9.99 us
    ppermute x2, starting transfers between devices, shards(): lax.ppermute(carried, 'rep', [(i, (i + away * columns) % replicas) for i...  6.58 us
    pallas_call x1, Pallas kernels, quantize(): pl.pallas_call(quantize_kernel, out_shape=jax.ShapeDtypeStruct(shape, jnp...  4.25 us
  transfers between devices with their start and end apart: 4, of which 2 were waited for; matrix products, arithmetic and copies ran while one was open for 2% of the time, Pallas kernels for 0%

profile of v7, /device:TPU:2, one launch (start us, length us, event | category | flops | bytes accessed | tf_op | source)
XLA Modules:
  0.0 106.3 jit_solution(8433067172576637159)
XLA Ops:
  0.6 4.3 %shard_map.67 = bf16[96,8192]{1,0:T(8,128)(2,1)} custom-call(bf16[96,8192]{1,0:T(8,128)(2,1)} %global_ref.1, bf16[96,8192]{1,0:T(8,128)(2,1)} %bitcast.11), custom_call_target="tpu_custom_call" | custom-call | tf_op jit(solution)/shard_map/pallas_call | solution.py:68
  4.9 0.0 copy-start.1
  4.9 33.1 %all_to_all.20.parts_ref = bf16[12,8,8192]{2,1,0:T(8,128)(2,1)S(1)} all-to-all(bf16[12,8,8192]{2,1,0:T(8,128)(2,1)} %bitcast.13), channel_id=1, replica_groups={{256,320,0,64,128,192,640,704,512,576,384,448},{257,321,1,65,129,193,64..., dimensions={0} | all-to-all | bytes 3145728 | tf_op jit(solution)/shard_map/all_to_all | solution.py:244
  38.0 0.0 copy-done.1
  38.0 0.8 shard_map.68
  38.8 15.2 %all-to-all-start.1 = ((f32[24,1,128]{2,1,0:T(1,128)}), f32[24,1,128]{2,1,0:T(1,128)S(1)}, u32[]{:S(2)}, u32[]{:S(2)}) async-start(f32[24,1,128]{2,1,0:T(1,128)} %get-tuple-element.12), calls=%async_computation.1 | async-start | bytes 24576 | tf_op jit(solution)/shard_map/all_to_all | solution.py:226
  54.0 4.7 %collective-permute-start.1 = (bf16[3,8,8192]{2,1,0:T(8,128)(2,1)S(1)}, bf16[3,8,8192]{2,1,0:T(8,128)(2,1)S(1)}, u32[]{:S(2)}, u32[]{:S(2)}) collective-permute-start(bf16[3,8,8192]{2,1,0:T(8,128)(2,1)S(1)} %get-tuple-element.13.own_ref), channel_id=1, source_target_pairs={{0,512},{64,576},{128,640},{192,704},{256,0},{320,64},{384,128},{4... | collective-permute-start | bytes 1179656 | tf_op jit(solution)/shard_map/ppermute | solution.py:249
  58.7 1.9 %collective-permute-start = (bf16[3,8,8192]{2,1,0:T(8,128)(2,1)S(1)}, bf16[3,8,8192]{2,1,0:T(8,128)(2,1)S(1)}, u32[]{:S(2)}, u32[]{:S(2)}) collective-permute-start(bf16[3,8,8192]{2,1,0:T(8,128)(2,1)S(1)} %get-tuple-element.13.own_ref), channel_id=1, source_target_pairs={{0,256},{64,320},{128,384},{192,448},{256,512},{320,576},{384,640}... | collective-permute-start | bytes 1179656 | tf_op jit(solution)/shard_map/ppermute | solution.py:249
  60.6 3.2 %all-to-all-done.1 = f32[24,1,128]{2,1,0:T(1,128)S(1)} async-done(((f32[24,1,128]{2,1,0:T(1,128)}), f32[24,1,128]{2,1,0:T(1,128)S(1)}, u32[]{:S(2)}, u32[]{:S(2)}) %all-to-all-start.1) | async-done | bytes 12320 | tf_op jit(solution)/shard_map/all_to_all | solution.py:226
  63.8 0.6 broadcast_in_dim.10
  64.4 8.7 %all-to-all-start.2 = ((f32[32,1,128]{2,1,0:T(1,128)}), f32[32,1,128]{2,1,0:T(1,128)S(1)}, u32[]{:S(2)}, u32[]{:S(2)}) async-start(f32[32,1,128]{2,1,0:T(1,128)} %broadcast_in_dim.10), calls=%async_computation.2 | async-start | bytes 32768 | tf_op jit(solution)/shard_map/all_to_all | solution.py:226
  73.1 1.0 dynamic-slice_bitcast_fusion.owned_ref
  74.8 6.8 %all-to-all-done.2.parts_ref = f32[32,1,128]{2,1,0:T(1,128)S(1)} async-done(((f32[32,1,128]{2,1,0:T(1,128)}), f32[32,1,128]{2,1,0:T(1,128)S(1)}, u32[]{:S(2)}, u32[]{:S(2)}) %all-to-all-start.2) | async-done | bytes 16416 | tf_op jit(solution)/shard_map/all_to_all | solution.py:226
  81.7 0.0 collective-permute-done.1.ahead_ref
  81.7 0.0 collective-permute-done.behind_ref
  81.7 0.5 shard_map.69
  82.2 0.0 copy-start
  82.2 22.1 %all_to_all.21.gathered_ref = bf16[4,3,8,8192]{3,2,1,0:T(8,128)(2,1)S(1)} all-to-all(bf16[4,3,8,8192]{3,2,1,0:T(8,128)(2,1)S(1)} %get-tuple-element.17), channel_id=1, replica_groups={{0,64,192,128},{256,320,448,384},{512,576,704,640},{1,65,193,129},{257,..., dimensions={0} | all-to-all | bytes 3145728 | tf_op jit(solution)/shard_map/all_to_all | solution.py:261
  104.3 0.0 copy-done
  104.3 2.0 %shard_map.70 = (bf16[12,8,8192]{2,1,0:T(8,128)(2,1)}, f32[8,8192]{1,0:T(8,128)}, bf16[12,8,8192]{2,1,0:T(8,128)(2,1)}) custom-call(f32[8,128]{1,0:T(8,128)S(1)} %get-tuple-element.14.alpha_ref, f32[8,128]{1,0:T(8,128)S(1)} %get-tuple-element.15.factor_ref, f32[8,8192]{1,0:T(8,128)S(1)} %get-tuple-element.16.average_ref, f32[8,8192]{1,0:T(8,128)S(1)} %copy-done.1, ...), custom_call_target="tpu_custom_call" | custom-call | tf_op jit(solution)/shard_map/pallas_call | solution.py:195
  (1 shorter events, 0.0 us)
Async XLA Ops:
  4.9 33.1 %copy-start.1 = (f32[8,8192]{1,0:T(8,128)S(1)}, f32[8,8192]{1,0:T(8,128)}, u32[]{:S(2)}) copy-start(f32[8,8192]{1,0:T(8,128)} %momentum_ref.3) | copy-start | bytes 786436
  38.8 24.9 %all-to-all-start.1 = ((f32[24,1,128]{2,1,0:T(1,128)}), f32[24,1,128]{2,1,0:T(1,128)S(1)}, u32[]{:S(2)}, u32[]{:S(2)}) async-start(f32[24,1,128]{2,1,0:T(1,128)} %get-tuple-element.12), calls=%async_computation.1 | async-start | bytes 24576 | tf_op jit(solution)/shard_map/all_to_all | solution.py:226
  54.0 27.7 %collective-permute-start.1 = (bf16[3,8,8192]{2,1,0:T(8,128)(2,1)S(1)}, bf16[3,8,8192]{2,1,0:T(8,128)(2,1)S(1)}, u32[]{:S(2)}, u32[]{:S(2)}) collective-permute-start(bf16[3,8,8192]{2,1,0:T(8,128)(2,1)S(1)} %get-tuple-element.13.own_ref), channel_id=1, source_target_pairs={{0,512},{64,576},{128,640},{192,704},{256,0},{320,64},{384,128},{4... | collective-permute-start | bytes 1179656 | tf_op jit(solution)/shard_map/ppermute | solution.py:249
  58.7 23.0 %collective-permute-start = (bf16[3,8,8192]{2,1,0:T(8,128)(2,1)S(1)}, bf16[3,8,8192]{2,1,0:T(8,128)(2,1)S(1)}, u32[]{:S(2)}, u32[]{:S(2)}) collective-permute-start(bf16[3,8,8192]{2,1,0:T(8,128)(2,1)S(1)} %get-tuple-element.13.own_ref), channel_id=1, source_target_pairs={{0,256},{64,320},{128,384},{192,448},{256,512},{320,576},{384,640}... | collective-permute-start | bytes 1179656 | tf_op jit(solution)/shard_map/ppermute | solution.py:249
  64.4 17.3 %all-to-all-start.2 = ((f32[32,1,128]{2,1,0:T(1,128)}), f32[32,1,128]{2,1,0:T(1,128)S(1)}, u32[]{:S(2)}, u32[]{:S(2)}) async-start(f32[32,1,128]{2,1,0:T(1,128)} %broadcast_in_dim.10), calls=%async_computation.2 | async-start | bytes 32768 | tf_op jit(solution)/shard_map/all_to_all | solution.py:226
  82.2 22.1 %copy-start = (bf16[1,96,8192]{2,1,0:T(8,128)(2,1)S(1)}, bf16[1,96,8192]{2,1,0:T(8,128)(2,1)}, u32[]{:S(2)}) copy-start(bf16[1,96,8192]{2,1,0:T(8,128)(2,1)} %param.5) | copy-start | bytes 4718596
